TPU v7x, 128 devices: a whole 4x4x4 slice. The times are simulated.
128 devices in a mesh: seq: 32 (over y, x, core), exp: 4 (over z).
Axes of the slice: x: 4, y: 4, z: 4, core: 2. Of those that a mesh axis runs over, the one named last changes fastest.
Arguments:
- stream: bfloat16 [16384, 4096], P(('exp', 'seq')), may hold values from -6 to 6
- query_input: bfloat16 [16384, 4096], P(('exp', 'seq')), may hold values from -9 to 9
- key_input: bfloat16 [16384, 4096], P(('exp', 'seq')), may hold values from -4.5 to 4.5
- value_input: bfloat16 [16384, 4096], P(('exp', 'seq')), may hold values from -12 to 12
- sample_id: int32 [16384], replicated, may hold values from 0 to 31, never falling along the last dimension, each value on 1 to 1024 neighbouring positions
- timestep: int32 [32], replicated, may hold values from 0 to 999
- class_id: int32 [32], replicated, may hold values from 0 to 999
- class_table: bfloat16 [1000, 4096], P(None, 'seq'), may hold values from -6 to 6
- mod_weight: bfloat16 [4096, 16384], P(None, ('seq', 'exp')), may hold values from -0.09375 to 0.09375
- router_weight: bfloat16 [4096, 32], replicated, may hold values from -0.09375 to 0.09375
- expert_in: bfloat16 [32, 4096, 4096], P('seq', None, 'exp'), may hold values from -0.09375 to 0.09375
- expert_out: bfloat16 [32, 4096, 4096], P('seq', 'exp'), may hold values from -0.09375 to 0.09375
- picked: int32 [32, 128, 2], P(None, ('exp', 'seq')), may hold values from 0 to 127, as said below
- counts: int32 [32, 128], P(None, ('exp', 'seq')), may hold values from 1 to 2, as said below
Outputs:
- block_output: bfloat16 [16384, 4096], P(('exp', 'seq'))
Inputs may be any that keep to these rules, and one draw needn't show every extreme that they name: For j < counts[e, b] the entries picked[e, b, j] are distinct; entries from counts[e, b] on are ignored. `counts`: in every draw one expert has 2 used slots in every block.
All inputs are finite; a program needn't handle non-finite values.
Results may differ from a plain program's by a relative error of at most 0.006.
Values may be sent and summed in bfloat16 or wider, within the bound.
A program may use at most 128 MiB of HBM per device.

v0:
```python
import math

import jax
import jax.numpy as jnp
from jax import lax
from jax.sharding import PartitionSpec as P

MOST = 1024


EPS = 1e-06


def with_halo(cells, sides, width):
    for axis, dim in sides:
        count = lax.axis_size(axis)
        ends = count - 1
        head = lax.slice_in_dim(cells, 0, width, axis=dim)
        tail = lax.slice_in_dim(cells, cells.shape[dim] - width, cells.shape[dim], axis=dim)
        cells = jnp.concatenate(
            [
                lax.ppermute(tail, axis, [(i, (i + 1) % count) for i in range(ends)]),
                cells,
                lax.ppermute(head, axis, [((i + 1) % count, i) for i in range(ends)]),
            ],
            axis=dim,
        )
    return cells


def local_attention(head_query, extended, query_ids, key_ids):
    group, head_width = head_query.shape
    q_block = min(512, group)
    key_span = q_block + 2 * MOST
    scale_factor = 1.0 / math.sqrt(head_width)

    def one_block(offset):
        query_part = lax.dynamic_slice_in_dim(head_query, offset, q_block, 0)
        window = lax.dynamic_slice_in_dim(extended, offset, key_span, 0)
        key_part = window[:, :head_width]
        value_part = window[:, head_width:]
        query_tags = lax.dynamic_slice_in_dim(query_ids, offset, q_block, 0)
        key_tags = lax.dynamic_slice_in_dim(key_ids, offset, key_span, 0)
        scores = (
            jnp.einsum("qd,kd->qk", query_part, key_part, preferred_element_type=jnp.float32)
            * scale_factor
        )
        allowed = query_tags[:, None] == key_tags[None, :]
        scores = jnp.where(allowed, scores, -1e30)
        highest = jnp.max(scores, axis=-1, keepdims=True)
        numer = jnp.where(allowed, jnp.exp(scores - highest), 0.0)
        denominator = jnp.sum(numer, axis=-1, keepdims=True)
        weights = (numer / denominator).astype(jnp.bfloat16)
        return jnp.dot(weights, value_part, preferred_element_type=jnp.float32).astype(jnp.bfloat16)

    offsets = jnp.arange(group // q_block, dtype=jnp.int32) * q_block
    return lax.map(one_block, offsets).reshape(group, head_width)


def on_device(
    stream,
    query_input,
    key_input,
    value_input,
    sample_id,
    timestep,
    class_id,
    class_table,
    mod_weight,
    router_weight,
    expert_in,
    expert_out,
    picked,
    counts,
):
    seq_count = lax.axis_size("seq")
    exp_count = lax.axis_size("exp")
    seq_index = lax.axis_index("seq")
    exp_index = lax.axis_index("exp")
    tok_local, width = stream.shape
    group = tok_local * seq_count
    owner_block = exp_index * seq_count + seq_index
    column_count = class_table.shape[1]
    half_width = width // 2
    column = seq_index * column_count + jnp.arange(column_count, dtype=jnp.int32)
    first_half = column < half_width
    freq_index = jnp.where(first_half, column, column - half_width).astype(jnp.float32)
    frequency = jnp.exp(-math.log(10000.0) * freq_index / half_width)
    angles = timestep.astype(jnp.float32)[:, None] * frequency[None, :]
    embedded = jnp.where(first_half[None, :], jnp.cos(angles), jnp.sin(angles))
    table_rows = jnp.take(class_table, class_id, axis=0).astype(jnp.float32)
    cond_columns = jax.nn.silu(embedded + table_rows).astype(jnp.bfloat16)
    condition = lax.all_gather(cond_columns, "seq", axis=1, tiled=True)
    local_mod = jnp.dot(condition, mod_weight, preferred_element_type=jnp.float32)
    modulation = lax.all_gather(local_mod, ("seq", "exp"), axis=1, tiled=True)
    head_query, head_key, head_value = (
        lax.all_to_all(query_input, "seq", split_axis=1, concat_axis=0, tiled=True),
        lax.all_to_all(key_input, "seq", split_axis=1, concat_axis=0, tiled=True),
        lax.all_to_all(value_input, "seq", split_axis=1, concat_axis=0, tiled=True),
    )
    key_value = jnp.concatenate([head_key, head_value], axis=1)
    extended = with_halo(key_value, (("exp", 0),), MOST)
    id_padded = jnp.pad(sample_id, (MOST, MOST), constant_values=-1)
    query_ids = lax.dynamic_slice_in_dim(sample_id, exp_index * group, group, 0)
    key_ids = lax.dynamic_slice_in_dim(id_padded, exp_index * group, group + 2 * MOST, 0)
    attended_head = local_attention(head_query, extended, query_ids, key_ids)
    attended = lax.all_to_all(attended_head, "seq", split_axis=0, concat_axis=1, tiled=True)
    own_ids = lax.dynamic_slice_in_dim(sample_id, owner_block * tok_local, tok_local, 0)
    selector = (
        own_ids[:, None] == jnp.arange(modulation.shape[0], dtype=jnp.int32)[None, :]
    ).astype(jnp.float32)
    token_mod = jnp.dot(selector, modulation, precision=lax.Precision.HIGHEST)
    gate_attn, shift, scale_mod, gate_ffn = jnp.split(token_mod, 4, axis=1)
    residual = stream.astype(jnp.float32) + gate_attn * attended.astype(jnp.float32)
    average = jnp.mean(residual, axis=1, keepdims=True)
    centered = residual - average
    variance = jnp.mean(centered * centered, axis=1, keepdims=True)
    normed = (centered * lax.rsqrt(variance + EPS) * (1.0 + scale_mod) + shift).astype(jnp.bfloat16)
    router = jax.nn.sigmoid(jnp.dot(normed, router_weight, preferred_element_type=jnp.float32))
    slots = picked[:, 0, :]
    expert_count, slot_total = slots.shape
    live = jnp.arange(slot_total, dtype=jnp.int32)[None, :] < counts[:, 0][:, None]
    chosen_rows = jnp.take(normed, slots.reshape(-1), axis=0).reshape(
        expert_count, slot_total, width
    )
    chosen_rows = jnp.where(live[:, :, None], chosen_rows, jnp.zeros((), jnp.bfloat16))
    w_first = expert_in[0]
    w_second = expert_out[0]
    collected = lax.all_gather(chosen_rows[None], "exp", axis=0, tiled=True)
    spread = lax.all_to_all(collected, "seq", split_axis=1, concat_axis=1, tiled=True)
    product = jnp.einsum(
        "rcd,df->rcf",
        spread.reshape(-1, slot_total, width),
        w_first,
        preferred_element_type=jnp.float32,
    )
    hidden = jax.nn.gelu(product, approximate=True).astype(jnp.bfloat16)
    hidden = hidden.reshape(-1, hidden.shape[-1])
    partial_rows = jnp.dot(hidden, w_second, preferred_element_type=jnp.float32)
    partial_rows = partial_rows.reshape(exp_count, seq_count, slot_total, width)
    arriving = lax.all_to_all(
        lax.all_to_all(
            partial_rows.astype(jnp.bfloat16), "seq", split_axis=1, concat_axis=1, tiled=True
        ),
        "exp",
        split_axis=0,
        concat_axis=0,
        tiled=True,
    ).astype(partial_rows.dtype)
    homeward = jnp.sum(arriving, axis=0).astype(jnp.bfloat16)
    placement = (slots[:, :, None] == jnp.arange(tok_local, dtype=jnp.int32)[None, None, :]) & live[
        :, :, None
    ]
    weighted = placement.astype(jnp.float32) * jnp.transpose(router)[:, None, :]
    expert_sum = jnp.einsum(
        "ect,ecd->td", weighted, homeward.astype(jnp.float32), precision=lax.Precision.HIGHEST
    )
    return (residual + gate_ffn * expert_sum).astype(jnp.bfloat16)


def solution(mesh):
    return jax.shard_map(
        on_device,
        mesh=mesh,
        in_specs=(
            P(("exp", "seq"), None),
            P(("exp", "seq"), None),
            P(("exp", "seq"), None),
            P(("exp", "seq"), None),
            P(),
            P(),
            P(),
            P(None, "seq"),
            P(None, ("seq", "exp")),
            P(),
            P("seq", None, "exp"),
            P("seq", "exp", None),
            P(None, ("exp", "seq"), None),
            P(None, ("exp", "seq")),
        ),
        out_specs=P(("exp", "seq"), None),
        check_vma=False,
    )
```

profile of v0, /device:TPU:1, one launch (start us, length us, event | category | flops | bytes accessed | tf_op | source)
XLA Modules:
  0.0 386.8 jit_solution(12971270141970663728)
XLA Ops:
  9.1 8.7 %all-to-all-start.1 = ((bf16[128,32,128]{2,0,1:T(8,128)(2,1)}), bf16[128,32,128]{2,0,1:T(8,128)(2,1)S(1)}, u32[]{:S(2)}, u32[]{:S(2)}) async-start(bf16[128,32,128]{2,0,1:T(8,128)(2,1)} %copy_bitcast_fusion.1), calls=%async_computation.1 | async-start | bytes 2097152 | tf_op jit(solution)/shard_map/all_to_all | solution.py:98
  19.1 15.9 %all-to-all-done.1 = bf16[128,32,128]{2,0,1:T(8,128)(2,1)S(1)} async-done(((bf16[128,32,128]{2,0,1:T(8,128)(2,1)}), bf16[128,32,128]{2,0,1:T(8,128)(2,1)S(1)}, u32[]{:S(2)}, u32[]{:S(2)}) %all-to-all-start.1) | async-done | bytes 1048608 | tf_op jit(solution)/shard_map/all_to_all | solution.py:98
  35.0 4.0 %all-to-all-start.2 = ((bf16[128,32,128]{2,0,1:T(8,128)(2,1)}), bf16[128,32,128]{2,0,1:T(8,128)(2,1)S(1)}, u32[]{:S(2)}, u32[]{:S(2)}) async-start(bf16[128,32,128]{2,0,1:T(8,128)(2,1)} %copy_bitcast_fusion), calls=%async_computation.2 | async-start | bytes 2097152 | tf_op jit(solution)/shard_map/all_to_all | solution.py:99
  39.0 1.6 gather_fusion
  40.8 31.8 %all_gather.9 = bf16[32,4096]{1,0:T(8,128)(2,1)S(1)} all-gather(bf16[32,128]{1,0:T(8,128)(2,1)S(1)} %multiply_convert_fusion), channel_id=1, replica_groups=mesh['seq'=32,'exp'=4] {'seq'}, dimensions={1}, use_global_device_ids=true | all-gather | bytes 270336 | tf_op jit(solution)/shard_map/all_gather | solution.py:93
  74.7 4.3 %collective-permute-start = (bf16[1024,256]{1,0:T(8,128)(2,1)}, bf16[1024,256]{1,0:T(8,128)(2,1)}, u32[]{:S(2)}, u32[]{:S(2)}) collective-permute-start(bf16[1024,256]{1,0:T(8,128)(2,1)} %get-tuple-element.61), channel_id=1, source_target_pairs={{0,1},{1,2},{2,3},{4,5},{5,6},{6,7},{8,9},{9,10},{10,11},{12,13},{... | collective-permute-start | bytes 1572872 | tf_op jit(solution)/shard_map/ppermute | solution.py:22
  81.6 4.8 %all-to-all-start = ((bf16[128,32,128]{2,0,1:T(8,128)(2,1)}), bf16[128,32,128]{2,0,1:T(8,128)(2,1)S(1)}, u32[]{:S(2)}, u32[]{:S(2)}) async-start(bf16[128,32,128]{2,0,1:T(8,128)(2,1)} %copy_bitcast_fusion.2), calls=%async_computation | async-start | bytes 2097152 | tf_op jit(solution)/shard_map/all_to_all | solution.py:97
  86.8 3.1 collective-permute-done
  89.8 4.6 %collective-permute-done.1 = bf16[1024,256]{1,0:T(8,128)(2,1)} collective-permute-done((bf16[1024,256]{1,0:T(8,128)(2,1)}, bf16[1024,256]{1,0:T(8,128)(2,1)}, u32[]{:S(2)}, u32[]{:S(2)}) %collective-permute-start.1) | collective-permute-done | bytes 524320 | tf_op jit(solution)/shard_map/ppermute | solution.py:24
  94.4 3.1 pad_maximum_fusion
  97.5 6.1 %all-to-all-done = bf16[128,32,128]{2,0,1:T(8,128)(2,1)S(1)} async-done(((bf16[128,32,128]{2,0,1:T(8,128)(2,1)}), bf16[128,32,128]{2,0,1:T(8,128)(2,1)S(1)}, u32[]{:S(2)}, u32[]{:S(2)}) %all-to-all-start) | async-done | bytes 1048608 | tf_op jit(solution)/shard_map/all_to_all | solution.py:97
  103.6 87.1 %while.10 = (s32[]{:T(128)}, bf16[8,512,128]{2,1,0:T(8,128)(2,1)}, s32[8]{0:T(128)S(1)}, s32[4096]{0:T(1024)S(1)}, s32[6144]{0:T(1024)S(1)}, /*index=5*/bf16[409...) while((s32[]{:T(128)}, bf16[8,512,128]{2,1,0:T(8,128)(2,1)}, ...), condition=%wide.region_3.4_spmd, body=%wide.region_0.3_spmd.sunk | while | flops 688192512 | bytes 17375468 | solution.py:57
  107.1 2.3 fusion.77
  110.5 4.0 %fusion.79 = bf16[8,512,128]{2,1,0:T(8,128)(2,1)} fusion(bf16[8,512,128]{2,1,0:T(8,128)(2,1)} %get-tuple-element.123, s32[]{:T(128)S(6)} %copy.72, f32[512,2560]{1,0:T(8,128)S(1)} %get-tuple-element.108, f32[512]{0:T(512)S(1)} %fusion.78, f32[512]{0:T(512)S(1)} %get-tuple-element.109, s32[2560]{0:T(1024)S(1)} %dynamic_slice.39, ...), kind=kOutput, calls=%fused_computation.9.clone.1 | convolution fusion | flops 342163456 | bytes 6045708 | tf_op jit(solution)/shard_map/while/body/eval_jaxpr/dot_general | solution.py:54
  118.0 2.3 fusion.77
  121.4 4.0 %fusion.79 = bf16[8,512,128]{2,1,0:T(8,128)(2,1)} fusion(bf16[8,512,128]{2,1,0:T(8,128)(2,1)} %get-tuple-element.123, s32[]{:T(128)S(6)} %copy.72, f32[512,2560]{1,0:T(8,128)S(1)} %get-tuple-element.108, f32[512]{0:T(512)S(1)} %fusion.78, f32[512]{0:T(512)S(1)} %get-tuple-element.109, s32[2560]{0:T(1024)S(1)} %dynamic_slice.39, ...), kind=kOutput, calls=%fused_computation.9.clone.1 | convolution fusion | flops 342163456 | bytes 6045708 | tf_op jit(solution)/shard_map/while/body/eval_jaxpr/dot_general | solution.py:54
  128.8 2.3 fusion.77
  132.3 4.0 %fusion.79 = bf16[8,512,128]{2,1,0:T(8,128)(2,1)} fusion(bf16[8,512,128]{2,1,0:T(8,128)(2,1)} %get-tuple-element.123, s32[]{:T(128)S(6)} %copy.72, f32[512,2560]{1,0:T(8,128)S(1)} %get-tuple-element.108, f32[512]{0:T(512)S(1)} %fusion.78, f32[512]{0:T(512)S(1)} %get-tuple-element.109, s32[2560]{0:T(1024)S(1)} %dynamic_slice.39, ...), kind=kOutput, calls=%fused_computation.9.clone.1 | convolution fusion | flops 342163456 | bytes 6045708 | tf_op jit(solution)/shard_map/while/body/eval_jaxpr/dot_general | solution.py:54
  139.7 2.3 fusion.77
  143.2 4.0 %fusion.79 = bf16[8,512,128]{2,1,0:T(8,128)(2,1)} fusion(bf16[8,512,128]{2,1,0:T(8,128)(2,1)} %get-tuple-element.123, s32[]{:T(128)S(6)} %copy.72, f32[512,2560]{1,0:T(8,128)S(1)} %get-tuple-element.108, f32[512]{0:T(512)S(1)} %fusion.78, f32[512]{0:T(512)S(1)} %get-tuple-element.109, s32[2560]{0:T(1024)S(1)} %dynamic_slice.39, ...), kind=kOutput, calls=%fused_computation.9.clone.1 | convolution fusion | flops 342163456 | bytes 6045708 | tf_op jit(solution)/shard_map/while/body/eval_jaxpr/dot_general | solution.py:54
  150.6 2.3 fusion.77
  154.1 4.0 %fusion.79 = bf16[8,512,128]{2,1,0:T(8,128)(2,1)} fusion(bf16[8,512,128]{2,1,0:T(8,128)(2,1)} %get-tuple-element.123, s32[]{:T(128)S(6)} %copy.72, f32[512,2560]{1,0:T(8,128)S(1)} %get-tuple-element.108, f32[512]{0:T(512)S(1)} %fusion.78, f32[512]{0:T(512)S(1)} %get-tuple-element.109, s32[2560]{0:T(1024)S(1)} %dynamic_slice.39, ...), kind=kOutput, calls=%fused_computation.9.clone.1 | convolution fusion | flops 342163456 | bytes 6045708 | tf_op jit(solution)/shard_map/while/body/eval_jaxpr/dot_general | solution.py:54
  161.5 2.3 fusion.77
  165.0 4.0 %fusion.79 = bf16[8,512,128]{2,1,0:T(8,128)(2,1)} fusion(bf16[8,512,128]{2,1,0:T(8,128)(2,1)} %get-tuple-element.123, s32[]{:T(128)S(6)} %copy.72, f32[512,2560]{1,0:T(8,128)S(1)} %get-tuple-element.108, f32[512]{0:T(512)S(1)} %fusion.78, f32[512]{0:T(512)S(1)} %get-tuple-element.109, s32[2560]{0:T(1024)S(1)} %dynamic_slice.39, ...), kind=kOutput, calls=%fused_computation.9.clone.1 | convolution fusion | flops 342163456 | bytes 6045708 | tf_op jit(solution)/shard_map/while/body/eval_jaxpr/dot_general | solution.py:54
  172.4 2.3 fusion.77
  175.9 4.0 %fusion.79 = bf16[8,512,128]{2,1,0:T(8,128)(2,1)} fusion(bf16[8,512,128]{2,1,0:T(8,128)(2,1)} %get-tuple-element.123, s32[]{:T(128)S(6)} %copy.72, f32[512,2560]{1,0:T(8,128)S(1)} %get-tuple-element.108, f32[512]{0:T(512)S(1)} %fusion.78, f32[512]{0:T(512)S(1)} %get-tuple-element.109, s32[2560]{0:T(1024)S(1)} %dynamic_slice.39, ...), kind=kOutput, calls=%fused_computation.9.clone.1 | convolution fusion | flops 342163456 | bytes 6045708 | tf_op jit(solution)/shard_map/while/body/eval_jaxpr/dot_general | solution.py:54
  183.3 2.3 fusion.77
  186.8 4.0 %fusion.79 = bf16[8,512,128]{2,1,0:T(8,128)(2,1)} fusion(bf16[8,512,128]{2,1,0:T(8,128)(2,1)} %get-tuple-element.123, s32[]{:T(128)S(6)} %copy.72, f32[512,2560]{1,0:T(8,128)S(1)} %get-tuple-element.108, f32[512]{0:T(512)S(1)} %fusion.78, f32[512]{0:T(512)S(1)} %get-tuple-element.109, s32[2560]{0:T(1024)S(1)} %dynamic_slice.39, ...), kind=kOutput, calls=%fused_computation.9.clone.1 | convolution fusion | flops 342163456 | bytes 6045708 | tf_op jit(solution)/shard_map/while/body/eval_jaxpr/dot_general | solution.py:54
  190.7 4.0 %all-to-all-start.3 = ((bf16[32,128,128]{2,1,0:T(8,128)(2,1)}), bf16[32,128,128]{2,1,0:T(8,128)(2,1)S(1)}, u32[]{:S(2)}, u32[]{:S(2)}) async-start(bf16[32,128,128]{2,1,0:T(8,128)(2,1)} %bitcast.91), calls=%async_computation.3 | async-start | bytes 2097152 | tf_op jit(solution)/shard_map/all_to_all | solution.py:107
  195.0 7.4 %fusion.42 = f32[128,16384]{1,0:T(8,128)} fusion(f32[32,16384]{1,0:T(8,128)} %all-gather.3.cloned.1.call-done, s32[128]{0:T(128)S(1)} %dynamic_slice.25), kind=kOutput, calls=%fused_computation.58 | convolution fusion | flops 805310464 | bytes 10486272 | tf_op jit(solution)/shard_map/dot_general | solution.py:112
  202.4 9.6 %all-to-all-done.3 = bf16[32,128,128]{2,1,0:T(8,128)(2,1)S(1)} async-done(((bf16[32,128,128]{2,1,0:T(8,128)(2,1)}), bf16[32,128,128]{2,1,0:T(8,128)(2,1)S(1)}, u32[]{:S(2)}, u32[]{:S(2)}) %all-to-all-start.3) | async-done | bytes 1048608 | tf_op jit(solution)/shard_map/all_to_all | solution.py:107
  212.0 2.4 fusion.59
  214.8 1.5 copy-done.2
  217.0 1.7 gather_fusion.1
  218.7 2.2 gather.12
  220.9 2.5 fusion.41
  223.4 30.3 %all-gather.5.cloned.1.call-done = bf16[4,32,2,4096]{3,1,2,0:T(8,128)(2,1)} async-done(((bf16[1,32,2,4096]{3,1,2,0:T(8,128)(2,1)}), bf16[4,32,2,4096]{3,1,2,0:T(8,128)(2,1)}) %all-gather.5.cloned.1.call-update) | async-done | bytes 2097168 | tf_op jit(solution)/shard_map/all_gather | solution.py:129
  253.7 3.2 copy.44
  256.9 35.7 %all_to_all.85 = bf16[4,32,2,4096]{3,0,2,1:T(4,128)(2,1)S(1)} all-to-all(bf16[4,32,2,4096]{3,0,2,1:T(4,128)(2,1)S(1)} %copy.44), channel_id=1, replica_groups=mesh['seq'=32,'exp'=4] {'seq'}, dimensions={1} | all-to-all | bytes 4194304 | tf_op jit(solution)/shard_map/all_to_all | solution.py:130
  293.8 6.1 %fusion.36 = bf16[128,2,1024]{2,0,1:T(8,128)(2,1)S(1)} fusion(bf16[128,2,4096]{2,0,1:T(8,128)(2,1)S(1)} %bitcast.89, bf16[1,4096,1024]{2,1,0:T(8,128)(2,1)} %param.26), kind=kOutput, calls=%fused_computation.46 | convolution fusion | flops 2149842944 | bytes 11010048 | tf_op jit(solution)/shard_map/rcd,df->rcf/dot_general | solution.py:131
  300.0 2.3 fusion.14
  302.4 2.2 copy.47
  304.6 31.9 %all_to_all.86 = bf16[4,32,2,4096]{3,2,0,1:T(2,128)(2,1)S(1)} all-to-all(bf16[4,32,2,4096]{3,2,0,1:T(2,128)(2,1)S(1)} %copy.47), channel_id=1, replica_groups=mesh['seq'=32,'exp'=4] {'seq'}, dimensions={1} | all-to-all | bytes 4194304 | tf_op jit(solution)/shard_map/all_to_all | solution.py:142
  336.5 3.3 copy.48
  339.8 4.9 %all-to-all-start.6 = ((bf16[4,32,2,4096]{3,2,1,0:T(2,128)(2,1)}), bf16[4,32,2,4096]{3,2,1,0:T(2,128)(2,1)}, u32[]{:S(2)}, u32[]{:S(2)}) async-start(bf16[4,32,2,4096]{3,2,1,0:T(2,128)(2,1)} %copy.48), calls=%async_computation.6 | async-start | bytes 4194304 | tf_op jit(solution)/shard_map/all_to_all | solution.py:141
  345.2 25.4 %all-to-all-done.6 = bf16[4,32,2,4096]{3,2,1,0:T(2,128)(2,1)} async-done(((bf16[4,32,2,4096]{3,2,1,0:T(2,128)(2,1)}), bf16[4,32,2,4096]{3,2,1,0:T(2,128)(2,1)}, u32[]{:S(2)}, u32[]{:S(2)}) %all-to-all-start.6) | async-done | bytes 2097184 | tf_op jit(solution)/shard_map/all_to_all | solution.py:141
  370.6 5.5 %reduce_sum.41 = bf16[32,2,4096]{2,1,0:T(2,128)(2,1)} reduce(bf16[4,32,2,4096]{3,2,1,0:T(2,128)(2,1)} %all-to-all-done.6, bf16[]{:T(256)} %constant.64.clone.1), dimensions={0}, to_apply=%region_6.7 | reduce | flops 786432 | bytes 2621442 | tf_op jit(solution)/shard_map/reduce_sum | solution.py:150
  376.1 3.9 %fusion.19 = bf16[128,4096]{1,0:T(8,128)(2,1)} fusion(f32[128,4096]{1,0:T(8,128)S(1)} %get-tuple-element.58, f32[128,16384]{1,0:T(8,128)} %fusion.42, bf16[32,2,4096]{2,1,0:T(2,128)(2,1)} %reduce_sum.41, f32[32,128]{1,0:T(8,128)S(1)} %fusion.26, s32[32,2]{0,1:T(2,128)S(1)} %bitcast.92, pred[32,2]{0,1:T(4,128)(4,1)S(1)} %iota_compare_fusion.3), kind=kOutput, calls=%fused_computation.23 | convolution fusion | flops 404250624 | bytes 5783872 | tf_op jit(solution)/shard_map/ect,ecd->td/dot_general | solution.py:155
  (97 shorter events, 26.8 us)
Async XLA Ops:
  6.5 1.2 copy-start
  6.5 11.3 %copy-start.10 = (s32[32]{0:T(128)S(1)}, s32[32]{0:T(128)}, u32[]{:S(2)}) copy-start(s32[32]{0:T(128)} %param.22) | copy-start | bytes 388
  6.5 11.3 %copy-start.3 = (bf16[128,4096]{1,0:T(8,128)(2,1)S(1)}, bf16[128,4096]{1,0:T(8,128)(2,1)}, u32[]{:S(2)}) copy-start(bf16[128,4096]{1,0:T(8,128)(2,1)} %param.19) | copy-start | bytes 3145732
  9.1 30.0 %copy-start.9 = (s32[32]{0:T(128)S(1)}, s32[32]{0:T(128)}, u32[]{:S(2)}) copy-start(s32[32]{0:T(128)} %param.21) | copy-start | bytes 388
  9.1 63.6 %copy-start.4 = (bf16[4096,128]{1,0:T(8,128)(2,1)S(1)}, bf16[4096,128]{1,0:T(8,128)(2,1)}, u32[]{:S(2)}) copy-start(bf16[4096,128]{1,0:T(8,128)(2,1)} %param.24) | copy-start | bytes 3145732
  9.1 25.9 %all-to-all-start.1 = ((bf16[128,32,128]{2,0,1:T(8,128)(2,1)}), bf16[128,32,128]{2,0,1:T(8,128)(2,1)S(1)}, u32[]{:S(2)}, u32[]{:S(2)}) async-start(bf16[128,32,128]{2,0,1:T(8,128)(2,1)} %copy_bitcast_fusion.1), calls=%async_computation.1 | async-start | bytes 2097152 | tf_op jit(solution)/shard_map/all_to_all | solution.py:98
  35.0 38.6 %all-to-all-start.2 = ((bf16[128,32,128]{2,0,1:T(8,128)(2,1)}), bf16[128,32,128]{2,0,1:T(8,128)(2,1)S(1)}, u32[]{:S(2)}, u32[]{:S(2)}) async-start(bf16[128,32,128]{2,0,1:T(8,128)(2,1)} %copy_bitcast_fusion), calls=%async_computation.2 | async-start | bytes 2097152 | tf_op jit(solution)/shard_map/all_to_all | solution.py:99
  39.0 156.1 %all-gather.3.cloned.1.call-start = ((), (), s32[]{:S(2)}) async-start(), calls=%async_computation.7 | async-start | bytes 2113536 | tf_op jit(solution)/shard_map/all_gather | solution.py:95
  73.5 6.8 %copy-start.5 = (bf16[128,4096]{1,0:T(8,128)(2,1)S(1)}, bf16[128,4096]{1,0:T(8,128)(2,1)}, u32[]{:S(2)}) copy-start(bf16[128,4096]{1,0:T(8,128)(2,1)} %param.17) | copy-start | bytes 3145732
  73.6 12.8 %copy-start.7 = (s32[16384]{0:T(1024)S(1)}, s32[16384]{0:T(1024)}, u32[]{:S(2)}) copy-start(s32[16384]{0:T(1024)} %param.20) | copy-start | bytes 196612
  73.6 12.9 %copy-start.8 = (s32[32,1,2]{0,2,1:T(2,128)S(1)}, s32[32,1,2]{0,2,1:T(2,128)}, u32[]{:S(2)}) copy-start(s32[32,1,2]{0,2,1:T(2,128)} %param.28) | copy-start | bytes 772
  74.7 15.1 %collective-permute-start = (bf16[1024,256]{1,0:T(8,128)(2,1)}, bf16[1024,256]{1,0:T(8,128)(2,1)}, u32[]{:S(2)}, u32[]{:S(2)}) collective-permute-start(bf16[1024,256]{1,0:T(8,128)(2,1)} %get-tuple-element.61), channel_id=1, source_target_pairs={{0,1},{1,2},{2,3},{4,5},{5,6},{6,7},{8,9},{9,10},{10,11},{12,13},{... | collective-permute-start | bytes 1572872 | tf_op jit(solution)/shard_map/ppermute | solution.py:22
  79.0 15.4 %collective-permute-start.1 = (bf16[1024,256]{1,0:T(8,128)(2,1)}, bf16[1024,256]{1,0:T(8,128)(2,1)}, u32[]{:S(2)}, u32[]{:S(2)}) collective-permute-start(bf16[1024,256]{1,0:T(8,128)(2,1)} %get-tuple-element.62), channel_id=1, source_target_pairs={{1,0},{2,1},{3,2},{5,4},{6,5},{7,6},{9,8},{10,9},{11,10},{13,12},{... | collective-permute-start | bytes 1572872 | tf_op jit(solution)/shard_map/ppermute | solution.py:24
  81.6 22.0 %all-to-all-start = ((bf16[128,32,128]{2,0,1:T(8,128)(2,1)}), bf16[128,32,128]{2,0,1:T(8,128)(2,1)S(1)}, u32[]{:S(2)}, u32[]{:S(2)}) async-start(bf16[128,32,128]{2,0,1:T(8,128)(2,1)} %copy_bitcast_fusion.2), calls=%async_computation | async-start | bytes 2097152 | tf_op jit(solution)/shard_map/all_to_all | solution.py:97
  86.7 16.9 %dynamic-slice-start = ((s32[16384]{0:T(1024)}, s32[]{:T(128)}), s32[4096]{0:T(1024)S(1)}, s32[]{:S(2)}) async-start(s32[16384]{0:T(1024)} %param.20, s32[]{:T(128)} %select_n.90), calls=%async_computation.9 | async-start | bytes 33280 | tf_op jit(solution)/shard_map/dynamic_slice | solution.py:104
  103.6 91.3 %copy-start.11 = (s32[32,1]{0,1:T(1,128)S(1)}, s32[32,1]{0,1:T(1,128)}, u32[]{:S(2)}) copy-start(s32[32,1]{0,1:T(1,128)} %param.29) | copy-start | bytes 388
  190.7 21.3 %all-to-all-start.3 = ((bf16[32,128,128]{2,1,0:T(8,128)(2,1)}), bf16[32,128,128]{2,1,0:T(8,128)(2,1)S(1)}, u32[]{:S(2)}, u32[]{:S(2)}) async-start(bf16[32,128,128]{2,1,0:T(8,128)(2,1)} %bitcast.91), calls=%async_computation.3 | async-start | bytes 2097152 | tf_op jit(solution)/shard_map/all_to_all | solution.py:107
  194.7 59.0 %all-gather.5.cloned.1.call-start = ((), (), s32[]{:S(2)}) async-start(), calls=%async_computation.8 | async-start | bytes 2621440 | tf_op jit(solution)/shard_map/all_gather | solution.py:129
  212.0 4.3 %copy-start.2 = (f32[128,16384]{1,0:T(8,128)S(1)}, f32[128,16384]{1,0:T(8,128)}, u32[]{:S(2)}) copy-start(f32[128,16384]{1,0:T(8,128)} %fusion.42) | copy-start | bytes 25165828
  292.7 7.3 %slice-start = ((s8[8388608]{0:T(1024)(128)(4,1)}), s8[4194304]{0:T(1024)(128)(4,1)S(1)}, s32[]{:S(2)}) async-start(s8[8388608]{0:T(1024)(128)(4,1)} %bitcast.93), calls=%async_computation.10 | async-start | bytes 8388608
  293.8 6.2 %slice-start.1 = ((s8[8388608]{0:T(1024)(128)(4,1)}), s8[4194304]{0:T(1024)(128)(4,1)S(1)}, s32[]{:S(2)}) async-start(s8[8388608]{0:T(1024)(128)(4,1)} %bitcast.93), calls=%async_computation.11 | async-start | bytes 8388608
  339.8 4.9 %copy-start.6 = (bf16[4096,32]{0,1:T(8,128)(2,1)S(1)}, bf16[4096,32]{0,1:T(8,128)(2,1)}, u32[]{:S(2)}) copy-start(bf16[4096,32]{0,1:T(8,128)(2,1)} %param.25) | copy-start | bytes 786436
  339.8 30.8 %all-to-all-start.6 = ((bf16[4,32,2,4096]{3,2,1,0:T(2,128)(2,1)}), bf16[4,32,2,4096]{3,2,1,0:T(2,128)(2,1)}, u32[]{:S(2)}, u32[]{:S(2)}) async-start(bf16[4,32,2,4096]{3,2,1,0:T(2,128)(2,1)} %copy.48), calls=%async_computation.6 | async-start | bytes 4194304 | tf_op jit(solution)/shard_map/all_to_all | solution.py:141
  370.6 9.4 %copy-start.1 = (bf16[128,4096]{1,0:T(8,128)(2,1)S(1)}, bf16[128,4096]{1,0:T(8,128)(2,1)}, u32[]{:S(2)}) copy-start(bf16[128,4096]{1,0:T(8,128)(2,1)} %param.18) | copy-start | bytes 3145732
Sparse Core Ops, SparseCore 0:
  73.7 67.3 all-gather.2
  223.5 30.1 all-gather.4
where the time goes:
time: 389 us; the launch traced here: 387 us
  blocking collectives  99.5 us (26%)
  waiting for transfers between devices  95 us (24%)
  matrix products  71.5 us (18%)
  starting transfers between devices  32.2 us (8%)
  local copies, waits for them, and re-layouts  27.8 us (7%)
  other arithmetic  25.2 us (6%)
  loops' own time  21.8 us (6%)
  between operations  13.8 us (4%)
    all_to_all x1, blocking collectives, on_device(): lax.all_to_all(collected, 'seq', split_axis=1, concat_axis=1, tiled=True)  35.7 us
    all_to_all x1, blocking collectives, on_device(): lax.all_to_all(partial_rows.astype(jnp.bfloat16), 'seq', split_axis=1, co...  31.9 us
    dot_general x8, matrix products, one_block(): jnp.dot(weights, value_part, preferred_element_type=jnp.float32)  31.9 us
    all_gather x1, blocking collectives, on_device(): condition = lax.all_gather(cond_columns, 'seq', axis=1, tiled=True)  31.8 us
    all_gather x1, waiting for transfers between devices, on_device(): collected = lax.all_gather(chosen_rows[None], 'exp', axis=0, tiled=True)  30.3 us
    all_to_all x1, waiting for transfers between devices, on_device(): lax.all_to_all(lax.all_to_all(partial_rows.astype(jnp.bfloat16), 'seq', s...  25.4 us
    another operation x1, loops' own time, local_attention(): return lax.map(one_block, offsets).reshape(group, head_width)  21.8 us
    dot_general x8, matrix products, one_block(): jnp.einsum('qd,kd->qk', query_part, key_part, preferred_element_type=jnp....  18.5 us
  transfers between devices with their start and end apart: 9, of which 7 were waited for; matrix products, arithmetic and copies ran while one was open for 21% of the time, Pallas kernels for 0%

commit v1 on v0

--- a/solution.py
+++ b/solution.py
@@ -3,6 +3,8 @@
 import jax
 import jax.numpy as jnp
 from jax import lax
+from jax.experimental import pallas as pl
+from jax.experimental.pallas import tpu as pltpu
 from jax.sharding import PartitionSpec as P
 
 MOST = 1024
@@ -28,33 +30,84 @@
     return cells
 
 
-def local_attention(head_query, extended, query_ids, key_ids):
+Q_ROWS = 256
+FAR = 32768.0
+
+
+def attention_kernel(spans, q_ref, fq_ref, k_ref, fk_ref, v_ref, out_ref):
+    step = pl.program_id(0)
+    start = spans[0, step]
+    parts = spans[1, step]
+    head_width = q_ref.shape[1]
+    factor = math.log2(math.e) / math.sqrt(head_width)
+    most_parts = (2 * MOST + Q_ROWS) // Q_ROWS + 1
+
+    def with_parts(number):
+        span = number * Q_ROWS
+
+        @pl.when(parts == number)
+        def _():
+            first = pl.multiple_of(jnp.minimum(start, k_ref.shape[0] - span), 128)
+            rows = pl.ds(first, span)
+            query = jnp.concatenate([q_ref[...], fq_ref[...]], axis=1)
+            keys = jnp.concatenate([k_ref[rows, :], fk_ref[rows, :]], axis=1)
+            scores = lax.dot_general(
+                query, keys, (((1,), (1,)), ((), ())), preferred_element_type=jnp.float32
+            )
+            highest = jnp.max(scores, axis=1, keepdims=True)
+            numer = jnp.exp2((scores - highest) * factor).astype(jnp.bfloat16)
+            values = jnp.concatenate(
+                [v_ref[rows, :], jnp.ones((span, head_width), jnp.bfloat16)], axis=1
+            )
+            total = jnp.dot(numer, values, preferred_element_type=jnp.float32)
+            out_ref[...] = (total[:, :head_width] / total[:, head_width:]).astype(jnp.bfloat16)
+
+    for number in range(2, most_parts + 1):
+        with_parts(number)
+
+
+def local_attention(head_query, keys, values, sample_id, exp_index):
     group, head_width = head_query.shape
-    q_block = min(512, group)
-    key_span = q_block + 2 * MOST
-    scale_factor = 1.0 / math.sqrt(head_width)
-
-    def one_block(offset):
-        query_part = lax.dynamic_slice_in_dim(head_query, offset, q_block, 0)
-        window = lax.dynamic_slice_in_dim(extended, offset, key_span, 0)
-        key_part = window[:, :head_width]
-        value_part = window[:, head_width:]
-        query_tags = lax.dynamic_slice_in_dim(query_ids, offset, q_block, 0)
-        key_tags = lax.dynamic_slice_in_dim(key_ids, offset, key_span, 0)
-        scores = (
-            jnp.einsum("qd,kd->qk", query_part, key_part, preferred_element_type=jnp.float32)
-            * scale_factor
-        )
-        allowed = query_tags[:, None] == key_tags[None, :]
-        scores = jnp.where(allowed, scores, -1e30)
-        highest = jnp.max(scores, axis=-1, keepdims=True)
-        numer = jnp.where(allowed, jnp.exp(scores - highest), 0.0)
-        denominator = jnp.sum(numer, axis=-1, keepdims=True)
-        weights = (numer / denominator).astype(jnp.bfloat16)
-        return jnp.dot(weights, value_part, preferred_element_type=jnp.float32).astype(jnp.bfloat16)
-
-    offsets = jnp.arange(group // q_block, dtype=jnp.int32) * q_block
-    return lax.map(one_block, offsets).reshape(group, head_width)
+    extent = keys.shape[0]
+    blocks = group // Q_ROWS
+    first_token = exp_index * group
+    images = jnp.arange(head_width, dtype=jnp.int32)[None, :]
+    query_ids = lax.dynamic_slice_in_dim(sample_id, first_token, group, 0)
+    id_padded = jnp.pad(sample_id, (MOST, MOST), constant_values=-1)
+    key_ids = lax.dynamic_slice_in_dim(id_padded, first_token, extent, 0)
+    query_tags = (query_ids[:, None] == images).astype(jnp.bfloat16)
+    key_tags = jnp.where(key_ids[:, None] == images, 0.0, -FAR).astype(jnp.bfloat16)
+    begins = jnp.sum(
+        (sample_id[None, :] < jnp.arange(33, dtype=jnp.int32)[:, None]).astype(jnp.int32), axis=1
+    )
+    by_block = query_ids.reshape(blocks, Q_ROWS)
+    shown = jnp.arange(33, dtype=jnp.int32)[None, :]
+    low = jnp.sum(jnp.where(by_block[:, :1] == shown, begins[None, :], 0), axis=1)
+    high = jnp.sum(jnp.where(by_block[:, -1:] + 1 == shown, begins[None, :], 0), axis=1)
+    low = (low - first_token + MOST) // 128 * 128
+    high = high - first_token + MOST
+    parts = jnp.maximum((high - low + Q_ROWS - 1) // Q_ROWS, 2)
+    spans = jnp.stack([low, parts]).astype(jnp.int32)
+    whole = lambda step, spans: (0, 0)
+    part = lambda step, spans: (step, 0)
+    return pl.pallas_call(
+        attention_kernel,
+        grid_spec=pltpu.PrefetchScalarGridSpec(
+            num_scalar_prefetch=1,
+            grid=(blocks,),
+            in_specs=[
+                pl.BlockSpec((Q_ROWS, head_width), part),
+                pl.BlockSpec((Q_ROWS, head_width), part),
+                pl.BlockSpec((extent, head_width), whole),
+                pl.BlockSpec((extent, head_width), whole),
+                pl.BlockSpec((extent, head_width), whole),
+            ],
+            out_specs=pl.BlockSpec((Q_ROWS, head_width), part),
+        ),
+        out_shape=jax.ShapeDtypeStruct((group, head_width), jnp.bfloat16),
+        compiler_params=pltpu.CompilerParams(vmem_limit_bytes=40 * 2**20),
+        name="attention",
+    )(spans, head_query, query_tags, keys, key_tags, values)
 
 
 def on_device(
@@ -98,12 +151,14 @@
         lax.all_to_all(key_input, "seq", split_axis=1, concat_axis=0, tiled=True),
         lax.all_to_all(value_input, "seq", split_axis=1, concat_axis=0, tiled=True),
     )
-    key_value = jnp.concatenate([head_key, head_value], axis=1)
-    extended = with_halo(key_value, (("exp", 0),), MOST)
-    id_padded = jnp.pad(sample_id, (MOST, MOST), constant_values=-1)
-    query_ids = lax.dynamic_slice_in_dim(sample_id, exp_index * group, group, 0)
-    key_ids = lax.dynamic_slice_in_dim(id_padded, exp_index * group, group + 2 * MOST, 0)
-    attended_head = local_attention(head_query, extended, query_ids, key_ids)
+    sides = (("exp", 0),)
+    attended_head = local_attention(
+        head_query,
+        with_halo(head_key, sides, MOST),
+        with_halo(head_value, sides, MOST),
+        sample_id,
+        exp_index,
+    )
     attended = lax.all_to_all(attended_head, "seq", split_axis=0, concat_axis=1, tiled=True)
     own_ids = lax.dynamic_slice_in_dim(sample_id, owner_block * tok_local, tok_local, 0)
     selector = (
@@ -126,8 +181,8 @@
     chosen_rows = jnp.where(live[:, :, None], chosen_rows, jnp.zeros((), jnp.bfloat16))
     w_first = expert_in[0]
     w_second = expert_out[0]
-    collected = lax.all_gather(chosen_rows[None], "exp", axis=0, tiled=True)
-    spread = lax.all_to_all(collected, "seq", split_axis=1, concat_axis=1, tiled=True)
+    arrived = lax.all_to_all(chosen_rows, "seq", split_axis=0, concat_axis=0, tiled=True)
+    spread = lax.all_gather(arrived, "exp", axis=0, tiled=True)
     product = jnp.einsum(
         "rcd,df->rcf",
         spread.reshape(-1, slot_total, width),
@@ -138,16 +193,11 @@
     hidden = hidden.reshape(-1, hidden.shape[-1])
     partial_rows = jnp.dot(hidden, w_second, preferred_element_type=jnp.float32)
     partial_rows = partial_rows.reshape(exp_count, seq_count, slot_total, width)
-    arriving = lax.all_to_all(
-        lax.all_to_all(
-            partial_rows.astype(jnp.bfloat16), "seq", split_axis=1, concat_axis=1, tiled=True
-        ),
-        "exp",
-        split_axis=0,
-        concat_axis=0,
-        tiled=True,
+    gathered = lax.all_to_all(
+        partial_rows.astype(jnp.bfloat16), "exp", split_axis=0, concat_axis=0, tiled=True
     ).astype(partial_rows.dtype)
-    homeward = jnp.sum(arriving, axis=0).astype(jnp.bfloat16)
+    summed = jnp.sum(gathered, axis=0).astype(jnp.bfloat16)
+    homeward = lax.all_to_all(summed, "seq", split_axis=0, concat_axis=0, tiled=True)
     placement = (slots[:, :, None] == jnp.arange(tok_local, dtype=jnp.int32)[None, None, :]) & live[
         :, :, None
     ]

time: 389 us -> 286 us (0.74)
  matrix products: 71.5 us -> 26.7 us
  blocking collectives: 99.5 us -> 69.9 us
  loops' own time: 21.8 us -> 0 us
  waiting for transfers between devices: 95 us -> 73.7 us
  Pallas kernels: 0 us -> 18 us
  starting transfers between devices: 32.2 us -> 40.5 us
  local copies, waits for them, and re-layouts: 27.8 us -> 22 us
  other arithmetic: 25.2 us -> 19.6 us
    dot_general x16 -> x0, matrix products: 50.3 us -> none  [the longest x8 31.9 us: one_block(): jnp.dot(weights, value_part, preferred_element_type=jnp.float32)]
    all_to_all x2, blocking collectives: 67.7 us -> 43.8 us  [the longest x1 28.7 us: on_device(): lax.all_to_all(partial_rows.astype(jnp.bfloat16), 'exp', split_axis=0, co...]
    another operation x1 -> x0, loops' own time: 21.8 us -> none  [local_attention(): return lax.map(one_block, offsets).reshape(group, head_width)]
    pallas_call x0 -> x1, Pallas kernels: none -> 18 us  [local_attention(): pl.pallas_call(attention_kernel, grid_spec=pltpu.PrefetchScalarGridSpec(n...]
    all_to_all x1, waiting for transfers between devices: 25.4 us -> 11 us  [on_device(): lax.all_to_all(summed, 'seq', split_axis=0, concat_axis=0, tiled=True)]
    reduce_sum x9 -> x3, other arithmetic: 14.8 us -> 2.57 us  [the longest x1 2.01 us: on_device(): summed = jnp.sum(gathered, axis=0).astype(jnp.bfloat16)]
    all_to_all x1, waiting for transfers between devices: 0.01 us -> 7.35 us  [on_device(): lax.all_to_all(value_input, 'seq', split_axis=1, concat_axis=0, tiled=True)]
    all_to_all x1, waiting for transfers between devices: 15.9 us -> 8.8 us  [on_device(): lax.all_to_all(key_input, 'seq', split_axis=1, concat_axis=0, tiled=True)]
  transfers between devices with their start and end apart: 9 -> 11, of which waited for: 7 -> 7; matrix products, arithmetic and copies ran while one was open for 21% -> 10% of each run, Pallas kernels for 0% -> 6%
where the time goes in v1:
time: 286 us; the launch traced here: 284 us
  waiting for transfers between devices  73.7 us (26%)
  blocking collectives  69.9 us (24%)
  starting transfers between devices  40.5 us (14%)
  matrix products  26.7 us (9%)
  local copies, waits for them, and re-layouts  22 us (8%)
  other arithmetic  19.6 us (7%)
  Pallas kernels  18 us (6%)
  between operations  13.7 us (5%)
    all_gather x1, waiting for transfers between devices, on_device(): spread = lax.all_gather(arrived, 'exp', axis=0, tiled=True)  30.3 us
    all_to_all x1, blocking collectives, on_device(): lax.all_to_all(partial_rows.astype(jnp.bfloat16), 'exp', split_axis=0, co...  28.7 us
    all_gather x1, blocking collectives, on_device(): condition = lax.all_gather(cond_columns, 'seq', axis=1, tiled=True)  26.2 us
    pallas_call x1, Pallas kernels, local_attention(): pl.pallas_call(attention_kernel, grid_spec=pltpu.PrefetchScalarGridSpec(n...  18 us
    all_to_all x1, blocking collectives, on_device(): lax.all_to_all(chosen_rows, 'seq', split_axis=0, concat_axis=0, tiled=True)  15.1 us
    all_to_all x1, waiting for transfers between devices, on_device(): lax.all_to_all(summed, 'seq', split_axis=0, concat_axis=0, tiled=True)  11 us
    all_to_all x1, waiting for transfers between devices, on_device(): lax.all_to_all(attended_head, 'seq', split_axis=0, concat_axis=1, tiled=T...  9.38 us
    all_to_all x1, waiting for transfers between devices, on_device(): lax.all_to_all(key_input, 'seq', split_axis=1, concat_axis=0, tiled=True)  8.8 us
  transfers between devices with their start and end apart: 11, of which 7 were waited for; matrix products, arithmetic and copies ran while one was open for 10% of the time, Pallas kernels for 6%

profile of v1, /device:TPU:1, one launch (start us, length us, event | category | flops | bytes accessed | tf_op | source)
XLA Modules:
  0.0 284.1 jit_solution(617657151845695640)
XLA Ops:
  6.5 0.7 compare_and_fusion.1
  8.6 1.6 gather_fusion
  10.3 26.2 %all_gather.9 = bf16[32,4096]{1,0:T(8,128)(2,1)S(1)} all-gather(bf16[32,128]{1,0:T(8,128)(2,1)S(1)} %multiply_convert_fusion), channel_id=1, replica_groups=mesh['seq'=32,'exp'=4] {'seq'}, dimensions={1}, use_global_device_ids=true | all-gather | bytes 270336 | tf_op jit(solution)/shard_map/all_gather | solution.py:146
  36.5 2.1 fusion.57
  38.7 1.3 copy_bitcast_fusion.1
  40.0 5.3 %all-to-all-start.1 = ((bf16[128,32,128]{2,0,1:T(8,128)(2,1)}), bf16[128,32,128]{2,0,1:T(8,128)(2,1)}, u32[]{:S(2)}, u32[]{:S(2)}) async-start(bf16[128,32,128]{2,0,1:T(8,128)(2,1)} %copy_bitcast_fusion.1), calls=%async_computation.1 | async-start | bytes 2097152 | tf_op jit(solution)/shard_map/all_to_all | solution.py:151
  45.9 2.8 select_convert_fusion.fk_ref
  49.0 2.5 copy_bitcast_fusion.2
  51.5 2.5 copy_bitcast_fusion
  54.0 8.8 %all-to-all-done.1 = bf16[128,32,128]{2,0,1:T(8,128)(2,1)} async-done(((bf16[128,32,128]{2,0,1:T(8,128)(2,1)}), bf16[128,32,128]{2,0,1:T(8,128)(2,1)}, u32[]{:S(2)}, u32[]{:S(2)}) %all-to-all-start.1) | async-done | bytes 1048608 | tf_op jit(solution)/shard_map/all_to_all | solution.py:151
  62.8 4.6 %all-to-all-start.2 = ((bf16[128,32,128]{2,0,1:T(8,128)(2,1)}), bf16[128,32,128]{2,0,1:T(8,128)(2,1)}, u32[]{:S(2)}, u32[]{:S(2)}) async-start(bf16[128,32,128]{2,0,1:T(8,128)(2,1)} %copy_bitcast_fusion), calls=%async_computation.2 | async-start | bytes 2097152 | tf_op jit(solution)/shard_map/all_to_all | solution.py:152
  67.5 2.7 fusion.13.fq_ref
  70.1 1.8 fusion.56
  71.9 1.3 collective-permute-start.1
  73.2 4.2 %collective-permute-start = (bf16[1024,128]{1,0:T(8,128)(2,1)S(1)}, bf16[1024,128]{1,0:T(8,128)(2,1)S(1)}, u32[]{:S(2)}, u32[]{:S(2)}) collective-permute-start(bf16[1024,128]{1,0:T(8,128)(2,1)S(1)} %bitcast.100), channel_id=1, source_target_pairs={{0,1},{1,2},{2,3},{4,5},{5,6},{6,7},{8,9},{9,10},{10,11},{12,13},{... | collective-permute-start | bytes 786440 | tf_op jit(solution)/shard_map/ppermute | solution.py:24
  77.8 7.4 %all-to-all-done.2 = bf16[128,32,128]{2,0,1:T(8,128)(2,1)} async-done(((bf16[128,32,128]{2,0,1:T(8,128)(2,1)}), bf16[128,32,128]{2,0,1:T(8,128)(2,1)}, u32[]{:S(2)}, u32[]{:S(2)}) %all-to-all-start.2) | async-done | bytes 1048608 | tf_op jit(solution)/shard_map/all_to_all | solution.py:152
  85.1 4.6 %all-to-all-start = ((bf16[128,32,128]{2,0,1:T(8,128)(2,1)}), bf16[128,32,128]{2,0,1:T(8,128)(2,1)}, u32[]{:S(2)}, u32[]{:S(2)}) async-start(bf16[128,32,128]{2,0,1:T(8,128)(2,1)} %copy_bitcast_fusion.2), calls=%async_computation | async-start | bytes 2097152 | tf_op jit(solution)/shard_map/all_to_all | solution.py:150
  89.8 1.1 fusion.55
  90.9 1.3 collective-permute-start.3
  92.2 4.4 %collective-permute-start.2 = (bf16[1024,128]{1,0:T(8,128)(2,1)S(1)}, bf16[1024,128]{1,0:T(8,128)(2,1)S(1)}, u32[]{:S(2)}, u32[]{:S(2)}) collective-permute-start(bf16[1024,128]{1,0:T(8,128)(2,1)S(1)} %bitcast.101), channel_id=1, source_target_pairs={{0,1},{1,2},{2,3},{4,5},{5,6},{6,7},{8,9},{9,10},{10,11},{12,13},{... | collective-permute-start | bytes 786440 | tf_op jit(solution)/shard_map/ppermute | solution.py:24
  96.6 2.5 pad_maximum_fusion.k_ref
  99.1 3.1 %collective-permute-done.3 = bf16[1024,128]{1,0:T(8,128)(2,1)S(1)} collective-permute-done((bf16[1024,128]{1,0:T(8,128)(2,1)S(1)}, bf16[1024,128]{1,0:T(8,128)(2,1)S(1)}, u32[]{:S(2)}, u32[]{:S(2)}) %collective-permute-start.3) | collective-permute-done | bytes 262176 | tf_op jit(solution)/shard_map/ppermute | solution.py:26
  102.1 2.5 pad_maximum_fusion.1.v_ref
  104.6 3.8 %all-to-all-done = bf16[128,32,128]{2,0,1:T(8,128)(2,1)} async-done(((bf16[128,32,128]{2,0,1:T(8,128)(2,1)}), bf16[128,32,128]{2,0,1:T(8,128)(2,1)}, u32[]{:S(2)}, u32[]{:S(2)}) %all-to-all-start) | async-done | bytes 1048608 | tf_op jit(solution)/shard_map/all_to_all | solution.py:150
  108.4 1.4 copy-done.1
  109.9 1.4 copy-done.2
  111.3 1.2 copy-done.3
  112.5 18.0 %attention.1 = bf16[4096,128]{1,0:T(8,128)(2,1)S(1)} custom-call(s32[2,16]{1,0:T(2,128)S(1)} %pad_add_fusion.spans, bf16[4096,128]{1,0:T(8,128)(2,1)} %bitcast.3.q_ref, bf16[4096,128]{1,0:T(8,128)(2,1)S(1)} %copy-done.3, bf16[6144,128]{1,0:T(8,128)(2,1)S(1)} %copy-done.1, bf16[6144,128]{1,0:T(8,128)(2,1)S(1)} %select_convert_fusion.fk_ref, ...), custom_call_target="tpu_custom_call" | custom-call | tf_op jit(solution)/shard_map/attention/pallas_call | solution.py:93
  130.5 1.0 copy-done.4
  131.4 5.8 %all-to-all-start.3 = ((bf16[32,128,128]{2,1,0:T(8,128)(2,1)}), bf16[32,128,128]{2,1,0:T(8,128)(2,1)S(1)}, u32[]{:S(2)}, u32[]{:S(2)}) async-start(bf16[32,128,128]{2,1,0:T(8,128)(2,1)} %bitcast.99), calls=%async_computation.3 | async-start | bytes 2097152 | tf_op jit(solution)/shard_map/all_to_all | solution.py:162
  137.6 7.4 %fusion.32 = f32[128,16384]{1,0:T(8,128)} fusion(f32[32,16384]{1,0:T(8,128)} %all-gather.3.cloned.1.call-done, s32[128]{0:T(128)S(1)} %dynamic_slice.9), kind=kOutput, calls=%fused_computation.50 | convolution fusion | flops 805310464 | bytes 10486272 | tf_op jit(solution)/shard_map/dot_general | solution.py:167
  145.0 9.4 %all-to-all-done.3 = bf16[32,128,128]{2,1,0:T(8,128)(2,1)S(1)} async-done(((bf16[32,128,128]{2,1,0:T(8,128)(2,1)}), bf16[32,128,128]{2,1,0:T(8,128)(2,1)S(1)}, u32[]{:S(2)}, u32[]{:S(2)}) %all-to-all-start.3) | async-done | bytes 1048608 | tf_op jit(solution)/shard_map/all_to_all | solution.py:162
  154.4 2.2 fusion.53
  157.0 1.0 copy-done.6
  158.0 1.2 copy-done.5
  159.9 0.9 gather_fusion.1
  161.1 0.7 broadcast_select_fusion.1
  161.8 15.1 %all_to_all.85 = bf16[32,2,4096]{2,1,0:T(2,128)(2,1)S(1)} all-to-all(bf16[32,2,4096]{2,1,0:T(2,128)(2,1)S(1)} %broadcast_select_fusion.1), channel_id=1, replica_groups=mesh['seq'=32,'exp'=4] {'seq'}, dimensions={0} | all-to-all | bytes 1048576 | tf_op jit(solution)/shard_map/all_to_all | solution.py:184
  176.9 1.1 copy.61
  178.0 30.3 %all-gather.5.cloned.1.call-done = bf16[128,2,4096]{2,0,1:T(8,128)(2,1)} async-done(((bf16[32,2,4096]{2,0,1:T(8,128)(2,1)}), bf16[128,2,4096]{2,0,1:T(8,128)(2,1)}) %all-gather.5.cloned.1.call-update) | async-done | bytes 2097168 | tf_op jit(solution)/shard_map/all_gather | solution.py:185
  208.3 6.6 %fusion.27 = bf16[128,2,1024]{2,0,1:T(8,128)(2,1)S(1)} fusion(bf16[128,2,4096]{2,0,1:T(8,128)(2,1)} %all-gather.5.cloned.1.call-done, bf16[1,4096,1024]{2,1,0:T(8,128)(2,1)} %param.24), kind=kOutput, calls=%fused_computation.40 | convolution fusion | flops 2149842944 | bytes 11010048 | tf_op jit(solution)/shard_map/rcd,df->rcf/dot_general | solution.py:186
  214.8 5.7 %fusion.4 = bf16[4,32,2,4096]{3,1,2,0:T(8,128)(2,1)S(1)} fusion(bf16[1,1024,4096]{2,1,0:T(8,128)(2,1)} %param.25, bf16[4,32,2,1024]{3,1,0,2:T(8,128)(2,1)S(1)} %bitcast.105), kind=kOutput, calls=%fused_computation.6 | convolution fusion | flops 2148532224 | bytes 11010048 | tf_op jit(solution)/shard_map/dot_general | solution.py:194
  220.6 28.7 %all_to_all.86 = bf16[4,32,2,4096]{3,1,2,0:T(8,128)(2,1)} all-to-all(bf16[4,32,2,4096]{3,1,2,0:T(8,128)(2,1)S(1)} %fusion.4), channel_id=1, replica_groups=mesh['seq'=32,'exp'=4] {'exp'}, dimensions={0} | all-to-all | bytes 4194304 | tf_op jit(solution)/shard_map/all_to_all | solution.py:196
  249.2 2.0 reduce_sum.62
  251.3 1.3 copy.63
  252.6 8.7 %all-to-all-start.6 = ((bf16[32,2,4096]{2,1,0:T(2,128)(2,1)}), bf16[32,2,4096]{2,1,0:T(2,128)(2,1)S(1)}, u32[]{:S(2)}, u32[]{:S(2)}) async-start(bf16[32,2,4096]{2,1,0:T(2,128)(2,1)} %copy.63), calls=%async_computation.6 | async-start | bytes 1048576 | tf_op jit(solution)/shard_map/all_to_all | solution.py:200
  261.9 11.0 %all-to-all-done.6 = bf16[32,2,4096]{2,1,0:T(2,128)(2,1)S(1)} async-done(((bf16[32,2,4096]{2,1,0:T(2,128)(2,1)}), bf16[32,2,4096]{2,1,0:T(2,128)(2,1)S(1)}, u32[]{:S(2)}, u32[]{:S(2)}) %all-to-all-start.6) | async-done | bytes 524320 | tf_op jit(solution)/shard_map/all_to_all | solution.py:200
  272.9 4.4 %fusion.9 = bf16[128,4096]{1,0:T(8,128)(2,1)} fusion(f32[128,4096]{1,0:T(8,128)} %copy-done.6, f32[128,16384]{1,0:T(8,128)} %fusion.32, bf16[32,2,4096]{2,1,0:T(2,128)(2,1)S(1)} %all-to-all-done.6, f32[32,128]{1,0:T(8,128)S(1)} %fusion.17, s32[32,2]{0,1:T(2,128)S(1)} %bitcast.103, pred[32,2]{0,1:T(4,128)(4,1)S(1)} %copy.58), kind=kOutput, calls=%fused_computation.10 | convolution fusion | flops 404250624 | bytes 5783872 | tf_op jit(solution)/shard_map/ect,ecd->td/dot_general | solution.py:205
  (55 shorter events, 5.0 us)
Async XLA Ops:
  6.5 32.1 %copy-start = (bf16[128,4096]{1,0:T(8,128)(2,1)S(1)}, bf16[128,4096]{1,0:T(8,128)(2,1)}, u32[]{:S(2)}) copy-start(bf16[128,4096]{1,0:T(8,128)(2,1)} %param.16) | copy-start | bytes 3145732
  6.5 131.1 %all-gather.3.cloned.1.call-start = ((), (), s32[]{:S(2)}) async-start(), calls=%async_computation.7 | async-start | bytes 2113536 | tf_op jit(solution)/shard_map/all_gather | solution.py:148
  38.7 6.6 %copy-start.8 = (s32[16384]{0:T(1024)S(1)}, s32[16384]{0:T(1024)}, u32[]{:S(2)}) copy-start(s32[16384]{0:T(1024)} %param.18) | copy-start | bytes 196612
  40.0 9.0 %copy-start.10 = (s32[32,1,2]{0,2,1:T(2,128)S(1)}, s32[32,1,2]{0,2,1:T(2,128)}, u32[]{:S(2)}) copy-start(s32[32,1,2]{0,2,1:T(2,128)} %param.26) | copy-start | bytes 772
  40.0 22.8 %all-to-all-start.1 = ((bf16[128,32,128]{2,0,1:T(8,128)(2,1)}), bf16[128,32,128]{2,0,1:T(8,128)(2,1)}, u32[]{:S(2)}, u32[]{:S(2)}) async-start(bf16[128,32,128]{2,0,1:T(8,128)(2,1)} %copy_bitcast_fusion.1), calls=%async_computation.1 | async-start | bytes 2097152 | tf_op jit(solution)/shard_map/all_to_all | solution.py:151
  62.8 22.3 %all-to-all-start.2 = ((bf16[128,32,128]{2,0,1:T(8,128)(2,1)}), bf16[128,32,128]{2,0,1:T(8,128)(2,1)}, u32[]{:S(2)}, u32[]{:S(2)}) async-start(bf16[128,32,128]{2,0,1:T(8,128)(2,1)} %copy_bitcast_fusion), calls=%async_computation.2 | async-start | bytes 2097152 | tf_op jit(solution)/shard_map/all_to_all | solution.py:152
  71.9 24.6 %collective-permute-start.1 = (bf16[1024,128]{1,0:T(8,128)(2,1)}, bf16[1024,128]{1,0:T(8,128)(2,1)S(1)}, u32[]{:S(2)}, u32[]{:S(2)}) collective-permute-start(bf16[1024,128]{1,0:T(8,128)(2,1)} %bitcast.7), channel_id=1, source_target_pairs={{1,0},{2,1},{3,2},{5,4},{6,5},{7,6},{9,8},{10,9},{11,10},{13,12},{... | collective-permute-start | bytes 786440 | tf_op jit(solution)/shard_map/ppermute | solution.py:26
  73.2 23.4 %collective-permute-start = (bf16[1024,128]{1,0:T(8,128)(2,1)S(1)}, bf16[1024,128]{1,0:T(8,128)(2,1)S(1)}, u32[]{:S(2)}, u32[]{:S(2)}) collective-permute-start(bf16[1024,128]{1,0:T(8,128)(2,1)S(1)} %bitcast.100), channel_id=1, source_target_pairs={{0,1},{1,2},{2,3},{4,5},{5,6},{6,7},{8,9},{9,10},{10,11},{12,13},{... | collective-permute-start | bytes 786440 | tf_op jit(solution)/shard_map/ppermute | solution.py:24
  85.1 23.3 %all-to-all-start = ((bf16[128,32,128]{2,0,1:T(8,128)(2,1)}), bf16[128,32,128]{2,0,1:T(8,128)(2,1)}, u32[]{:S(2)}, u32[]{:S(2)}) async-start(bf16[128,32,128]{2,0,1:T(8,128)(2,1)} %copy_bitcast_fusion.2), calls=%async_computation | async-start | bytes 2097152 | tf_op jit(solution)/shard_map/all_to_all | solution.py:150
  90.9 11.3 %collective-permute-start.3 = (bf16[1024,128]{1,0:T(8,128)(2,1)S(1)}, bf16[1024,128]{1,0:T(8,128)(2,1)S(1)}, u32[]{:S(2)}, u32[]{:S(2)}) collective-permute-start(bf16[1024,128]{1,0:T(8,128)(2,1)S(1)} %bitcast.102), channel_id=1, source_target_pairs={{1,0},{2,1},{3,2},{5,4},{6,5},{7,6},{9,8},{10,9},{11,10},{13,12},{... | collective-permute-start | bytes 786440 | tf_op jit(solution)/shard_map/ppermute | solution.py:26
  92.2 10.0 %collective-permute-start.2 = (bf16[1024,128]{1,0:T(8,128)(2,1)S(1)}, bf16[1024,128]{1,0:T(8,128)(2,1)S(1)}, u32[]{:S(2)}, u32[]{:S(2)}) collective-permute-start(bf16[1024,128]{1,0:T(8,128)(2,1)S(1)} %bitcast.101), channel_id=1, source_target_pairs={{0,1},{1,2},{2,3},{4,5},{5,6},{6,7},{8,9},{9,10},{10,11},{12,13},{... | collective-permute-start | bytes 786440 | tf_op jit(solution)/shard_map/ppermute | solution.py:24
  108.4 1.4 copy-start.1
  109.9 1.4 copy-start.2
  111.3 1.2 copy-start.3
  130.5 1.0 copy-start.4
  131.4 6.1 %copy-start.11 = (s32[32,1]{0,1:T(1,128)S(1)}, s32[32,1]{0,1:T(1,128)}, u32[]{:S(2)}) copy-start(s32[32,1]{0,1:T(1,128)} %param.27) | copy-start | bytes 388
  131.4 23.0 %all-to-all-start.3 = ((bf16[32,128,128]{2,1,0:T(8,128)(2,1)}), bf16[32,128,128]{2,1,0:T(8,128)(2,1)S(1)}, u32[]{:S(2)}, u32[]{:S(2)}) async-start(bf16[32,128,128]{2,1,0:T(8,128)(2,1)} %bitcast.99), calls=%async_computation.3 | async-start | bytes 2097152 | tf_op jit(solution)/shard_map/all_to_all | solution.py:162
  137.2 71.1 %all-gather.5.cloned.1.call-start = ((), (), s32[]{:S(2)}) async-start(), calls=%async_computation.8 | async-start | bytes 2621440 | tf_op jit(solution)/shard_map/all_gather | solution.py:185
  137.6 16.8 %copy-start.7 = (bf16[128,4096]{1,0:T(8,128)(2,1)S(1)}, bf16[128,4096]{1,0:T(8,128)(2,1)}, u32[]{:S(2)}) copy-start(bf16[128,4096]{1,0:T(8,128)(2,1)} %param.14) | copy-start | bytes 3145732
  154.4 4.8 %copy-start.5 = (f32[128,16384]{1,0:T(8,128)S(1)}, f32[128,16384]{1,0:T(8,128)}, u32[]{:S(2)}) copy-start(f32[128,16384]{1,0:T(8,128)} %fusion.32) | copy-start | bytes 25165828
  156.6 1.4 copy-start.6
  249.2 12.1 %copy-start.9 = (bf16[4096,32]{0,1:T(8,128)(2,1)S(1)}, bf16[4096,32]{0,1:T(8,128)(2,1)}, u32[]{:S(2)}) copy-start(bf16[4096,32]{0,1:T(8,128)(2,1)} %param.23) | copy-start | bytes 786436
  252.6 20.2 %all-to-all-start.6 = ((bf16[32,2,4096]{2,1,0:T(2,128)(2,1)}), bf16[32,2,4096]{2,1,0:T(2,128)(2,1)S(1)}, u32[]{:S(2)}, u32[]{:S(2)}) async-start(bf16[32,2,4096]{2,1,0:T(2,128)(2,1)} %copy.63), calls=%async_computation.6 | async-start | bytes 1048576 | tf_op jit(solution)/shard_map/all_to_all | solution.py:200
Sparse Core Ops, SparseCore 0:
  38.8 74.4 all-gather.2
  178.1 30.1 all-gather.4

commit v2 on v1

--- a/solution.py
+++ b/solution.py
@@ -110,6 +110,463 @@
     )(spans, head_query, query_tags, keys, key_tags, values)
 
 
+MESH = pl.DeviceIdType.MESH
+PLANE = 32
+TILE = 256
+PIECES = 8
+HALF = TILE * PIECES
+SLOT_ROWS = 64
+
+
+def shifted(place, offset, sign):
+    high = (place // 8 + sign * (offset // 8) + 4) % 4
+    middle = (place // 2 % 4 + sign * (offset // 2 % 4) + 4) % 4
+    return high * 8 + middle * 2 + (place + offset) % 2
+
+
+def for_offsets(body):
+    def step(index, carry):
+        body((index * 13) % PLANE)
+        return carry
+
+    lax.fori_loop(1, PLANE, step, 0)
+
+
+def greet(seq_index, exp_index, ring):
+    barrier = pltpu.get_barrier_semaphore()
+
+    def hello(offset):
+        pl.semaphore_signal(
+            barrier,
+            inc=1,
+            device_id=(shifted(seq_index, offset, 1), exp_index),
+            device_id_type=MESH,
+        )
+
+    for_offsets(hello)
+    for other in ring:
+        pl.semaphore_signal(barrier, inc=1, device_id=(seq_index, other), device_id_type=MESH)
+    pl.semaphore_wait(barrier, PLANE - 1 + len(ring))
+
+
+def rows_of(number, size):
+    return pl.ds(pl.multiple_of(number * size, size), size)
+
+
+def experts_kernel(
+    attended_ref,
+    stream_in,
+    modulation_in,
+    w_first_in,
+    w_second_in,
+    selector_ref,
+    target_ref,
+    placement_ref,
+    router_ref,
+    out_ref,
+    stream_ref,
+    modulation_ref,
+    w_first,
+    w_second,
+    attended,
+    token_mod,
+    residual,
+    normed,
+    pick,
+    unmix,
+    mix,
+    outgoing,
+    landed,
+    gathered,
+    lined,
+    hidden,
+    far_out,
+    far_in,
+    side_raw,
+    side_sum,
+    raw_in,
+    sum_in,
+    held,
+    own_total,
+    homeward,
+    back,
+    local_sem,
+    a_send,
+    a_recv,
+    d_send,
+    d_recv,
+    z_send,
+    z_recv,
+    r_send,
+    r_recv,
+    b_send,
+    b_recv,
+):
+    seq_index = lax.axis_index("seq")
+    exp_index = lax.axis_index("exp")
+    right = (exp_index + 1) % 4
+    left = (exp_index + 3) % 4
+    width = stream_ref.shape[1]
+    tokens = stream_ref.shape[0]
+    f32 = jnp.float32
+    bf16 = jnp.bfloat16
+
+    greet(seq_index, exp_index, (left, right))
+
+    def plane_copy(source, target, send, recv, peer):
+        return pltpu.make_async_remote_copy(
+            src_ref=source,
+            dst_ref=target,
+            send_sem=send,
+            recv_sem=recv,
+            device_id=(peer, exp_index),
+            device_id_type=MESH,
+        )
+
+    def ring_copy(source, target, send, recv, other):
+        return pltpu.make_async_remote_copy(
+            src_ref=source,
+            dst_ref=target,
+            send_sem=send,
+            recv_sem=recv,
+            device_id=(seq_index, other),
+            device_id_type=MESH,
+        )
+
+    def attended_copy(offset):
+        peer = shifted(seq_index, offset, 1)
+        return plane_copy(
+            attended_ref.at[rows_of(peer, tokens)],
+            attended.at[seq_index],
+            a_send.at[offset],
+            a_recv.at[offset],
+            peer,
+        )
+
+    for_offsets(lambda offset: attended_copy(offset).start())
+    own_attended = pltpu.make_async_copy(
+        attended_ref.at[rows_of(seq_index, tokens)], attended.at[seq_index], local_sem.at[0]
+    )
+    own_attended.start()
+    load_mod = pltpu.make_async_copy(modulation_in, modulation_ref, local_sem.at[1])
+    load_mod.start()
+    load_stream = pltpu.make_async_copy(stream_in, stream_ref, local_sem.at[2])
+    load_stream.start()
+    load_first = pltpu.make_async_copy(w_first_in.at[0], w_first, local_sem.at[3])
+    load_first.start()
+    load_second = pltpu.make_async_copy(w_second_in.at[0], w_second, local_sem.at[4])
+    load_second.start()
+
+    count = PIECES * SLOT_ROWS
+    row = lax.broadcasted_iota(jnp.int32, (count, count), 0)
+    column = lax.broadcasted_iota(jnp.int32, (count, count), 1)
+    by_source = ((row >> 1) & 31) * 16 + (row >> 6) * 2 + (row & 1)
+    unmix[...] = jnp.where(by_source == column, 1.0, 0.0).astype(bf16)
+    by_piece = ((row >> 1) & 7) * SLOT_ROWS + (row >> 4) * 2 + (row & 1)
+    mix[...] = jnp.where(by_piece == column, 1.0, 0.0).astype(bf16)
+    column = lax.broadcasted_iota(jnp.int32, pick.shape, 1)
+    pick[...] = jnp.where(target_ref[...] == column, 1.0, 0.0).astype(bf16)
+
+    load_mod.wait()
+    load_stream.wait()
+
+    def spread_mod(step, carry):
+        columns = rows_of(step, 512)
+        whole = modulation_ref[:, columns]
+        first = whole.astype(bf16)
+        rest = whole - first.astype(f32)
+        second = rest.astype(bf16)
+        third = (rest - second.astype(f32)).astype(bf16)
+        token_mod[:, columns] = jnp.dot(
+            selector_ref[...],
+            jnp.concatenate([first, second, third], axis=0),
+            preferred_element_type=f32,
+        )
+        return carry
+
+    lax.fori_loop(0, 4 * width // 512, spread_mod, 0)
+
+    own_attended.wait()
+    for_offsets(lambda offset: attended_copy(offset).wait_recv())
+
+    def norm_rows(step, carry):
+        rows = rows_of(step, 16)
+        heads = jnp.concatenate([attended[head, rows, :] for head in range(PLANE)], axis=1)
+        value = stream_ref[rows, :].astype(f32) + token_mod[rows, :width] * heads.astype(f32)
+        residual[rows, :] = value
+        average = jnp.mean(value, axis=1, keepdims=True)
+        centered = value - average
+        variance = jnp.mean(centered * centered, axis=1, keepdims=True)
+        shift = token_mod[rows, width : 2 * width]
+        scale = token_mod[rows, 2 * width : 3 * width]
+        normed[rows, :] = (centered * lax.rsqrt(variance + EPS) * (1.0 + scale) + shift).astype(bf16)
+        return carry
+
+    lax.fori_loop(0, tokens // 16, norm_rows, 0)
+
+    def dispatch_copy(half, offset):
+        peer = shifted(seq_index, offset, 1)
+        return plane_copy(
+            outgoing.at[half, rows_of(peer, 16)],
+            landed.at[half, rows_of(seq_index, 16)],
+            d_send.at[half, offset],
+            d_recv.at[half, offset],
+            peer,
+        )
+
+    for half in range(2):
+        stacked = jnp.concatenate(
+            [
+                normed[:, half * HALF + piece * TILE : half * HALF + (piece + 1) * TILE]
+                for piece in range(PIECES)
+            ],
+            axis=0,
+        )
+        outgoing[half] = jnp.dot(pick[...], stacked, preferred_element_type=f32).astype(bf16)
+        for_offsets(lambda offset: dispatch_copy(half, offset).start())
+        landed[half, rows_of(seq_index, 16), :] = outgoing[half, rows_of(seq_index, 16), :]
+
+    logits = jnp.dot(normed[...], router_ref[...], preferred_element_type=f32)
+    weighted = placement_ref[...] / (1.0 + jnp.exp(-logits))
+    weight_first = weighted.astype(bf16)
+    weight_rest = weighted - weight_first.astype(f32)
+    weight_second = weight_rest.astype(bf16)
+    weight_third = (weight_rest - weight_second.astype(f32)).astype(bf16)
+    weight_parts = jnp.concatenate([weight_first, weight_second, weight_third], axis=1)
+
+    def line_up(which, half):
+        lined[which * SLOT_ROWS : (which + 1) * SLOT_ROWS, half * HALF : (half + 1) * HALF] = (
+            jnp.concatenate(
+                [
+                    gathered[which, half, piece * SLOT_ROWS : (piece + 1) * SLOT_ROWS, :]
+                    for piece in range(PIECES)
+                ],
+                axis=1,
+            )
+        )
+
+    for half in range(2):
+        for_offsets(lambda offset: dispatch_copy(half, offset).wait_recv())
+        gathered[0, half] = jnp.dot(
+            unmix[...], landed[half], preferred_element_type=f32
+        ).astype(bf16)
+        if half == 0:
+            own_right_0 = ring_copy(
+                gathered.at[0, 0], gathered.at[2, 0], z_send.at[0], z_recv.at[0], right
+            )
+            own_right_0.start()
+        else:
+            own_left_1 = ring_copy(
+                gathered.at[0, 1], gathered.at[3, 1], z_send.at[1], z_recv.at[1], left
+            )
+            own_left_1.start()
+        line_up(0, half)
+    own_right_0.wait_recv()
+    on_right_0 = ring_copy(
+        gathered.at[2, 0], gathered.at[1, 0], z_send.at[2], z_recv.at[2], right
+    )
+    on_right_0.start()
+    own_left_1.wait_recv()
+    on_left_1 = ring_copy(gathered.at[3, 1], gathered.at[1, 1], z_send.at[3], z_recv.at[3], left)
+    on_left_1.start()
+    own_right_1 = ring_copy(
+        gathered.at[0, 1], gathered.at[2, 1], z_send.at[4], z_recv.at[4], right
+    )
+    own_right_1.start()
+    own_left_0 = ring_copy(gathered.at[0, 0], gathered.at[3, 0], z_send.at[5], z_recv.at[5], left)
+    own_left_0.start()
+    line_up(2, 0)
+    line_up(3, 1)
+    load_first.wait()
+    load_second.wait()
+
+    def first_product(base):
+        rows = slice(base, base + 2 * SLOT_ROWS)
+
+        def columns_of(step, carry):
+            columns = rows_of(step, 256)
+            product = jnp.dot(lined[rows, :], w_first[:, columns], preferred_element_type=f32)
+            hidden[rows, columns] = jax.nn.gelu(product, approximate=True).astype(bf16)
+            return carry
+
+        lax.fori_loop(0, w_first.shape[1] // 256, columns_of, 0)
+
+    def second_product(base, half, lower, upper):
+        rows = slice(base, base + 2 * SLOT_ROWS)
+
+        def columns_of(step, carry):
+            columns = rows_of(step, 256)
+            product = jnp.dot(
+                hidden[rows, :],
+                w_second[:, rows_of(step + half * (HALF // 256), 256)],
+                preferred_element_type=f32,
+            )
+            lower[:, columns] = product[:SLOT_ROWS].astype(lower.dtype)
+            upper[:, columns] = product[SLOT_ROWS:].astype(upper.dtype)
+            return carry
+
+        lax.fori_loop(0, HALF // 256, columns_of, 0)
+
+    on_right_0.wait_recv()
+    line_up(1, 0)
+    on_left_1.wait_recv()
+    line_up(1, 1)
+    first_product(0)
+    second_product(0, 0, own_total.at[0], far_out.at[0])
+    far_right = ring_copy(far_out.at[0], far_in.at[0], r_send.at[0], r_recv.at[0], right)
+    far_right.start()
+    second_product(0, 1, own_total.at[1], far_out.at[1])
+    far_left = ring_copy(far_out.at[1], far_in.at[1], r_send.at[1], r_recv.at[1], left)
+    far_left.start()
+    own_right_1.wait_recv()
+    line_up(2, 1)
+    own_left_0.wait_recv()
+    line_up(3, 0)
+    first_product(2 * SLOT_ROWS)
+    second_product(2 * SLOT_ROWS, 0, side_raw.at[0], held.at[0])
+    raw_left = ring_copy(side_raw.at[0], raw_in.at[0], r_send.at[2], r_recv.at[2], left)
+    raw_left.start()
+    second_product(2 * SLOT_ROWS, 1, held.at[1], side_raw.at[1])
+    raw_right = ring_copy(side_raw.at[1], raw_in.at[1], r_send.at[3], r_recv.at[3], right)
+    raw_right.start()
+    far_right.wait_recv()
+    side_sum[0] = (held[0] + far_in[0].astype(f32)).astype(bf16)
+    sum_right = ring_copy(side_sum.at[0], sum_in.at[0], r_send.at[4], r_recv.at[4], right)
+    sum_right.start()
+    far_left.wait_recv()
+    side_sum[1] = (held[1] + far_in[1].astype(f32)).astype(bf16)
+    sum_left = ring_copy(side_sum.at[1], sum_in.at[1], r_send.at[5], r_recv.at[5], left)
+    sum_left.start()
+
+    def return_copy(half, offset):
+        peer = shifted(seq_index, offset, 1)
+        return plane_copy(
+            homeward.at[half, rows_of(peer, 16)],
+            back.at[half, rows_of(seq_index, 16)],
+            b_send.at[half, offset],
+            b_recv.at[half, offset],
+            peer,
+        )
+
+    for half, raw, summed in ((0, raw_left, sum_right), (1, raw_right, sum_left)):
+        raw.wait_recv()
+        summed.wait_recv()
+        total = (
+            own_total[half] + raw_in[half].astype(f32) + sum_in[half].astype(f32)
+        ).astype(bf16)
+        stacked = jnp.concatenate(
+            [total[:, piece * TILE : (piece + 1) * TILE] for piece in range(PIECES)], axis=0
+        )
+        homeward[half] = jnp.dot(mix[...], stacked, preferred_element_type=f32).astype(bf16)
+        for_offsets(lambda offset: return_copy(half, offset).start())
+        back[half, rows_of(seq_index, 16), :] = homeward[half, rows_of(seq_index, 16), :]
+
+    for half in range(2):
+        for_offsets(lambda offset: return_copy(half, offset).wait_recv())
+        ordered = jnp.dot(unmix[...], back[half], preferred_element_type=f32).astype(bf16)
+        for piece in range(PIECES):
+            rows = ordered[piece * SLOT_ROWS : (piece + 1) * SLOT_ROWS, :]
+            begin = half * HALF + piece * TILE
+            columns = slice(begin, begin + TILE)
+            expert_sum = jnp.dot(
+                weight_parts, jnp.concatenate([rows, rows, rows], axis=0), preferred_element_type=f32
+            )
+            gate = token_mod[:, 3 * width + begin : 3 * width + begin + TILE]
+            out_ref[:, columns] = (residual[:, columns] + gate * expert_sum).astype(bf16)
+
+    for_offsets(lambda offset: attended_copy(offset).wait_send())
+    for half in range(2):
+        for_offsets(lambda offset: dispatch_copy(half, offset).wait_send())
+        for_offsets(lambda offset: return_copy(half, offset).wait_send())
+    for copy in (
+        own_right_0,
+        own_left_1,
+        on_right_0,
+        on_left_1,
+        own_right_1,
+        own_left_0,
+        far_right,
+        far_left,
+        raw_left,
+        raw_right,
+        sum_right,
+        sum_left,
+    ):
+        copy.wait_send()
+
+
+def feed_forward(
+    attended_head, stream, modulation, expert_in, expert_out, selector, target, placement, router
+):
+    tokens, width = stream.shape
+    bf16 = jnp.bfloat16
+    f32 = jnp.float32
+    part = expert_in.shape[2]
+    block = PIECES * SLOT_ROWS
+    anywhere = pl.BlockSpec(memory_space=pl.ANY)
+    inside = pl.BlockSpec(memory_space=pltpu.VMEM)
+    dma = pltpu.SemaphoreType.DMA
+    return pl.pallas_call(
+        experts_kernel,
+        out_shape=jax.ShapeDtypeStruct((tokens, width), bf16),
+        in_specs=[anywhere] * 5 + [inside] * 4,
+        out_specs=inside,
+        scratch_shapes=[
+            pltpu.VMEM((tokens, width), bf16),
+            pltpu.VMEM(modulation.shape, f32),
+            pltpu.VMEM((width, part), bf16),
+            pltpu.VMEM((part, width), bf16),
+            pltpu.VMEM((PLANE, tokens, width // PLANE), bf16),
+            pltpu.VMEM((tokens, 4 * width), f32),
+            pltpu.VMEM((tokens, width), f32),
+            pltpu.VMEM((tokens, width), bf16),
+            pltpu.VMEM((block, PIECES * tokens), bf16),
+            pltpu.VMEM((block, block), bf16),
+            pltpu.VMEM((block, block), bf16),
+            pltpu.VMEM((2, block, TILE), bf16),
+            pltpu.VMEM((2, block, TILE), bf16),
+            pltpu.VMEM((4, 2, block, TILE), bf16),
+            pltpu.VMEM((4 * SLOT_ROWS, width), bf16),
+            pltpu.VMEM((4 * SLOT_ROWS, part), bf16),
+            pltpu.VMEM((2, SLOT_ROWS, HALF), bf16),
+            pltpu.VMEM((2, SLOT_ROWS, HALF), bf16),
+            pltpu.VMEM((2, SLOT_ROWS, HALF), bf16),
+            pltpu.VMEM((2, SLOT_ROWS, HALF), bf16),
+            pltpu.VMEM((2, SLOT_ROWS, HALF), bf16),
+            pltpu.VMEM((2, SLOT_ROWS, HALF), bf16),
+            pltpu.VMEM((2, SLOT_ROWS, HALF), f32),
+            pltpu.VMEM((2, SLOT_ROWS, HALF), f32),
+            pltpu.VMEM((2, block, TILE), bf16),
+            pltpu.VMEM((2, block, TILE), bf16),
+            dma((5,)),
+            dma((PLANE,)),
+            dma((PLANE,)),
+            dma((2, PLANE)),
+            dma((2, PLANE)),
+            dma((6,)),
+            dma((6,)),
+            dma((6,)),
+            dma((6,)),
+            dma((2, PLANE)),
+            dma((2, PLANE)),
+        ],
+        compiler_params=pltpu.CompilerParams(
+            collective_id=1, has_side_effects=True, vmem_limit_bytes=58 * 2**20
+        ),
+        name="experts",
+    )(
+        attended_head,
+        stream,
+        modulation,
+        expert_in,
+        expert_out,
+        selector,
+        target,
+        placement,
+        router,
+    )
+
+
 def on_device(
     stream,
     query_input,
@@ -127,7 +584,6 @@
     counts,
 ):
     seq_count = lax.axis_size("seq")
-    exp_count = lax.axis_size("exp")
     seq_index = lax.axis_index("seq")
     exp_index = lax.axis_index("exp")
     tok_local, width = stream.shape
@@ -159,53 +615,31 @@
         sample_id,
         exp_index,
     )
-    attended = lax.all_to_all(attended_head, "seq", split_axis=0, concat_axis=1, tiled=True)
     own_ids = lax.dynamic_slice_in_dim(sample_id, owner_block * tok_local, tok_local, 0)
+    samples = modulation.shape[0]
     selector = (
-        own_ids[:, None] == jnp.arange(modulation.shape[0], dtype=jnp.int32)[None, :]
-    ).astype(jnp.float32)
-    token_mod = jnp.dot(selector, modulation, precision=lax.Precision.HIGHEST)
-    gate_attn, shift, scale_mod, gate_ffn = jnp.split(token_mod, 4, axis=1)
-    residual = stream.astype(jnp.float32) + gate_attn * attended.astype(jnp.float32)
-    average = jnp.mean(residual, axis=1, keepdims=True)
-    centered = residual - average
-    variance = jnp.mean(centered * centered, axis=1, keepdims=True)
-    normed = (centered * lax.rsqrt(variance + EPS) * (1.0 + scale_mod) + shift).astype(jnp.bfloat16)
-    router = jax.nn.sigmoid(jnp.dot(normed, router_weight, preferred_element_type=jnp.float32))
+        own_ids[:, None] == jnp.arange(3 * samples, dtype=jnp.int32)[None, :] % samples
+    ).astype(jnp.bfloat16)
     slots = picked[:, 0, :]
     expert_count, slot_total = slots.shape
     live = jnp.arange(slot_total, dtype=jnp.int32)[None, :] < counts[:, 0][:, None]
-    chosen_rows = jnp.take(normed, slots.reshape(-1), axis=0).reshape(
-        expert_count, slot_total, width
-    )
-    chosen_rows = jnp.where(live[:, :, None], chosen_rows, jnp.zeros((), jnp.bfloat16))
-    w_first = expert_in[0]
-    w_second = expert_out[0]
-    arrived = lax.all_to_all(chosen_rows, "seq", split_axis=0, concat_axis=0, tiled=True)
-    spread = lax.all_gather(arrived, "exp", axis=0, tiled=True)
-    product = jnp.einsum(
-        "rcd,df->rcf",
-        spread.reshape(-1, slot_total, width),
-        w_first,
-        preferred_element_type=jnp.float32,
-    )
-    hidden = jax.nn.gelu(product, approximate=True).astype(jnp.bfloat16)
-    hidden = hidden.reshape(-1, hidden.shape[-1])
-    partial_rows = jnp.dot(hidden, w_second, preferred_element_type=jnp.float32)
-    partial_rows = partial_rows.reshape(exp_count, seq_count, slot_total, width)
-    gathered = lax.all_to_all(
-        partial_rows.astype(jnp.bfloat16), "exp", split_axis=0, concat_axis=0, tiled=True
-    ).astype(partial_rows.dtype)
-    summed = jnp.sum(gathered, axis=0).astype(jnp.bfloat16)
-    homeward = lax.all_to_all(summed, "seq", split_axis=0, concat_axis=0, tiled=True)
-    placement = (slots[:, :, None] == jnp.arange(tok_local, dtype=jnp.int32)[None, None, :]) & live[
-        :, :, None
-    ]
-    weighted = placement.astype(jnp.float32) * jnp.transpose(router)[:, None, :]
-    expert_sum = jnp.einsum(
-        "ect,ecd->td", weighted, homeward.astype(jnp.float32), precision=lax.Precision.HIGHEST
-    )
-    return (residual + gate_ffn * expert_sum).astype(jnp.bfloat16)
+    chosen = jnp.where(live, slots, -1)
+    piece = jnp.arange(PIECES, dtype=jnp.int32)[None, :, None]
+    target = jnp.where(live[:, None, :], slots[:, None, :] + piece * tok_local, -1).reshape(-1, 1)
+    placement = (
+        chosen.reshape(1, -1) == jnp.arange(tok_local, dtype=jnp.int32)[:, None]
+    ).astype(jnp.float32)
+    return feed_forward(
+        attended_head,
+        stream,
+        modulation,
+        expert_in,
+        expert_out,
+        selector,
+        target,
+        placement,
+        jnp.repeat(router_weight, slot_total, axis=1),
+    )
 
 
 def solution(mesh):

time: 286 us -> 229 us (0.80)
  Pallas kernels: 18 us -> 109 us
  waiting for transfers between devices: 73.7 us -> 9.08 us
  blocking collectives: 69.9 us -> 31.6 us
  matrix products: 26.7 us -> 0.89 us
  starting transfers between devices: 40.5 us -> 28.3 us
  other arithmetic: 19.6 us -> 13.1 us
    pallas_call x0 -> x1, Pallas kernels: none -> 92.5 us  [feed_forward(): pl.pallas_call(experts_kernel, out_shape=jax.ShapeDtypeStruct((tokens, wi...]
    all_to_all x2 -> x0, blocking collectives: 43.8 us -> none  [the longest x1 28.7 us: on_device(): lax.all_to_all(partial_rows.astype(jnp.bfloat16), 'exp', split_axis=0, co...]
    all_gather x1 -> x0, waiting for transfers between devices: 30.3 us -> none  [on_device(): spread = lax.all_gather(arrived, 'exp', axis=0, tiled=True)]
    dot_general x5 -> x0, matrix products: 24.5 us -> none  [the longest x1 7.41 us: on_device(): token_mod = jnp.dot(selector, modulation, precision=lax.Precision.HIGHEST)]
    all_to_all x2 -> x0, waiting for transfers between devices: 20.4 us -> none  [the longest x1 11 us: on_device(): lax.all_to_all(summed, 'seq', split_axis=0, concat_axis=0, tiled=True)]
    all_to_all x2 -> x0, starting transfers between devices: 14.5 us -> none  [the longest x1 8.69 us: on_device(): lax.all_to_all(summed, 'seq', split_axis=0, concat_axis=0, tiled=True)]
    all_to_all x1, waiting for transfers between devices: 7.35 us -> 0.01 us  [on_device(): lax.all_to_all(value_input, 'seq', split_axis=1, concat_axis=0, tiled=True)]
    all_to_all x1, waiting for transfers between devices: 8.8 us -> 3.14 us  [on_device(): lax.all_to_all(key_input, 'seq', split_axis=1, concat_axis=0, tiled=True)]
  transfers between devices with their start and end apart: 11 -> 8, of which waited for: 7 -> 4; matrix products, arithmetic and copies ran while one was open for 10% -> 11% of each run, Pallas kernels for 6% -> 7%
where the time goes in v2:
time: 229 us; the launch traced here: 228 us
  Pallas kernels  109 us (48%)
  blocking collectives  31.6 us (14%)
  starting transfers between devices  28.3 us (12%)
  local copies, waits for them, and re-layouts  22.2 us (10%)
  between operations  13.7 us (6%)
  other arithmetic  13.1 us (6%)
  waiting for transfers between devices  9.08 us (4%)
    pallas_call x1, Pallas kernels, feed_forward(): pl.pallas_call(experts_kernel, out_shape=jax.ShapeDtypeStruct((tokens, wi...  92.5 us
    all_gather x1, blocking collectives, on_device(): condition = lax.all_gather(cond_columns, 'seq', axis=1, tiled=True)  31.6 us
    pallas_call x1, Pallas kernels, local_attention(): pl.pallas_call(attention_kernel, grid_spec=pltpu.PrefetchScalarGridSpec(n...  16.9 us
    unnamed x30, local copies, waits for them, and re-layouts  8.76 us
    all_to_all x1, starting transfers between devices, on_device(): lax.all_to_all(value_input, 'seq', split_axis=1, concat_axis=0, tiled=True)  8.64 us
    ppermute x2, starting transfers between devices, with_halo(): lax.ppermute(tail, axis, [(i, (i + 1) % count) for i in range(ends)])  7.76 us
    concatenate x2, other arithmetic, with_halo(): jnp.concatenate([lax.ppermute(tail, axis, [(i, (i + 1) % count) for i in...  5.05 us
    all_to_all x1, starting transfers between devices, on_device(): lax.all_to_all(key_input, 'seq', split_axis=1, concat_axis=0, tiled=True)  4.69 us
  transfers between devices with their start and end apart: 8, of which 4 were waited for; matrix products, arithmetic and copies ran while one was open for 11% of the time, Pallas kernels for 7%

profile of v2, /device:TPU:1, one launch (start us, length us, event | category | flops | bytes accessed | tf_op | source)
XLA Modules:
  0.0 228.3 jit_solution(3171477221138823906)
XLA Ops:
  6.6 1.2 copy-done
  7.8 1.3 copy_bitcast_fusion
  9.0 8.6 %all-to-all-start.2 = ((bf16[128,32,128]{2,0,1:T(8,128)(2,1)}), bf16[128,32,128]{2,0,1:T(8,128)(2,1)}, u32[]{:S(2)}, u32[]{:S(2)}) async-start(bf16[128,32,128]{2,0,1:T(8,128)(2,1)} %copy_bitcast_fusion), calls=%async_computation.2 | async-start | bytes 2097152 | tf_op jit(solution)/shard_map/all_to_all | solution.py:608
  17.9 1.6 gather_fusion
  19.4 0.1 multiply_convert_fusion
  19.6 31.6 %all_gather.6 = bf16[32,4096]{1,0:T(8,128)(2,1)S(1)} all-gather(bf16[32,128]{1,0:T(8,128)(2,1)S(1)} %multiply_convert_fusion), channel_id=1, replica_groups=mesh['seq'=32,'exp'=4] {'seq'}, dimensions={1}, use_global_device_ids=true | all-gather | bytes 270336 | tf_op jit(solution)/shard_map/all_gather | solution.py:602
  51.2 0.9 fusion.14
  52.2 0.4 convert_reduce_fusion
  52.6 0.2 slice_reduce_fusion
  52.8 1.3 copy_bitcast_fusion.1
  54.1 1.3 copy_bitcast_fusion.2
  55.3 0.1 dynamic_slice.11
  55.4 0.1 iota_compare_fusion.4
  55.5 0.1 copy.39
  55.6 0.1 copy.38
  55.7 0.1 lt.83
  55.8 0.1 squeeze.3
  55.9 0.6 fusion.1.placement_ref
  56.5 0.2 select_reduce_fusion.1
  56.7 0.7 compare_convert_fusion.selector_ref
  57.4 0.1 add_select_fusion
  57.5 2.8 %select_convert_fusion.fk_ref = bf16[6144,128]{1,0:T(8,128)(2,1)S(1)} fusion(s32[6144]{0:T(1024)S(1)} %pad_dynamic-slice_fusion), kind=kLoop, calls=%fused_computation.1 | loop fusion | flops 2359296 | bytes 1597440 | tf_op jit(solution)/shard_map/convert_element_type | solution.py:79
  60.4 4.7 %all-to-all-start.1 = ((bf16[128,32,128]{2,0,1:T(8,128)(2,1)}), bf16[128,32,128]{2,0,1:T(8,128)(2,1)}, u32[]{:S(2)}, u32[]{:S(2)}) async-start(bf16[128,32,128]{2,0,1:T(8,128)(2,1)} %copy_bitcast_fusion.1), calls=%async_computation.1 | async-start | bytes 2097152 | tf_op jit(solution)/shard_map/all_to_all | solution.py:607
  65.1 2.7 %fusion.fq_ref = bf16[4096,128]{1,0:T(8,128)(2,1)} fusion(s32[4096]{0:T(1024)S(1)} %dynamic_slice.9), kind=kLoop, calls=%fused_computation.6 | loop fusion | flops 1048576 | bytes 1064960 | tf_op jit(solution)/shard_map/convert_element_type | solution.py:78
  67.8 1.9 fusion.12
  69.7 3.5 %collective-permute-start.2 = (bf16[1024,128]{1,0:T(8,128)(2,1)}, bf16[1024,128]{1,0:T(8,128)(2,1)S(1)}, u32[]{:S(2)}, u32[]{:S(2)}) collective-permute-start(bf16[1024,128]{1,0:T(8,128)(2,1)} %bitcast.9), channel_id=1, source_target_pairs={{0,1},{1,2},{2,3},{4,5},{5,6},{6,7},{8,9},{9,10},{10,11},{12,13},{... | collective-permute-start | bytes 786440 | tf_op jit(solution)/shard_map/ppermute | solution.py:24
  73.2 1.3 collective-permute-start.3
  74.6 0.8 select_n.117.target_ref
  75.4 1.3 broadcast_in_dim.91
  76.7 1.2 reshape.272
  77.9 1.4 copy.41.router_ref
  79.3 3.1 %all-to-all-done.1 = bf16[128,32,128]{2,0,1:T(8,128)(2,1)} async-done(((bf16[128,32,128]{2,0,1:T(8,128)(2,1)}), bf16[128,32,128]{2,0,1:T(8,128)(2,1)}, u32[]{:S(2)}, u32[]{:S(2)}) %all-to-all-start.1) | async-done | bytes 1048608 | tf_op jit(solution)/shard_map/all_to_all | solution.py:607
  82.4 4.6 %all-to-all-start = ((bf16[128,32,128]{2,0,1:T(8,128)(2,1)}), bf16[128,32,128]{2,0,1:T(8,128)(2,1)}, u32[]{:S(2)}, u32[]{:S(2)}) async-start(bf16[128,32,128]{2,0,1:T(8,128)(2,1)} %copy_bitcast_fusion.2), calls=%async_computation | async-start | bytes 2097152 | tf_op jit(solution)/shard_map/all_to_all | solution.py:606
  87.0 1.1 fusion.13
  88.1 4.2 %collective-permute-start = (bf16[1024,128]{1,0:T(8,128)(2,1)S(1)}, bf16[1024,128]{1,0:T(8,128)(2,1)S(1)}, u32[]{:S(2)}, u32[]{:S(2)}) collective-permute-start(bf16[1024,128]{1,0:T(8,128)(2,1)S(1)} %bitcast.57), channel_id=1, source_target_pairs={{0,1},{1,2},{2,3},{4,5},{5,6},{6,7},{8,9},{9,10},{10,11},{12,13},{... | collective-permute-start | bytes 786440 | tf_op jit(solution)/shard_map/ppermute | solution.py:24
  92.3 1.3 collective-permute-start.1
  93.7 2.6 %pad_maximum_fusion.1.v_ref = bf16[6144,128]{1,0:T(8,128)(2,1)} fusion(bf16[1024,128]{1,0:T(8,128)(2,1)} %collective-permute-done.3, bf16[4096,128]{1,0:T(8,128)(2,1)} %bitcast.10, bf16[1024,128]{1,0:T(8,128)(2,1)S(1)} %collective-permute-done.2), kind=kLoop, calls=%fused_computation.8 | loop fusion | flops 4718592 | bytes 3145728 | tf_op jit(solution)/shard_map/concatenate | solution.py:22
  96.2 1.5 collective-permute-done
  97.8 4.2 %collective-permute-done.1 = bf16[1024,128]{1,0:T(8,128)(2,1)S(1)} collective-permute-done((bf16[1024,128]{1,0:T(8,128)(2,1)S(1)}, bf16[1024,128]{1,0:T(8,128)(2,1)S(1)}, u32[]{:S(2)}, u32[]{:S(2)}) %collective-permute-start.1) | collective-permute-done | bytes 262176 | tf_op jit(solution)/shard_map/ppermute | solution.py:26
  102.0 2.5 %pad_maximum_fusion.k_ref = bf16[6144,128]{1,0:T(8,128)(2,1)} fusion(bf16[1024,128]{1,0:T(8,128)(2,1)S(1)} %collective-permute-done.1, bf16[4096,128]{1,0:T(8,128)(2,1)} %bitcast.6, bf16[1024,128]{1,0:T(8,128)(2,1)S(1)} %collective-permute-done), kind=kLoop, calls=%fused_computation.7 | loop fusion | flops 4718592 | bytes 3145728 | tf_op jit(solution)/shard_map/concatenate | solution.py:22
  104.4 0.2 all-to-all-done
  104.6 1.4 copy-done.1
  106.0 1.5 copy-done.2
  107.6 1.2 copy-done.4
  108.8 16.9 %attention.1.attended_ref = bf16[4096,128]{1,0:T(8,128)(2,1)S(1)} custom-call(s32[2,16]{1,0:T(2,128)S(1)} %pad_add_fusion.spans, bf16[4096,128]{1,0:T(8,128)(2,1)} %bitcast.3.q_ref, bf16[4096,128]{1,0:T(8,128)(2,1)S(1)} %copy-done.4, bf16[6144,128]{1,0:T(8,128)(2,1)S(1)} %copy-done.2, bf16[6144,128]{1,0:T(8,128)(2,1)S(1)} %select_convert_fusion.fk_ref, ...), custom_call_target="tpu_custom_call" | custom-call | tf_op jit(solution)/shard_map/attention/pallas_call | solution.py:93
  125.7 1.0 copy-done.3
  126.7 92.5 %experts.1 = bf16[128,4096]{1,0:T(8,128)(2,1)} custom-call(bf16[4096,128]{1,0:T(8,128)(2,1)} %copy-done.3, bf16[128,4096]{1,0:T(8,128)(2,1)} %stream_in.1, f32[32,16384]{1,0:T(8,128)} %all-gather.2.cloned.1.call-done.modulation_in, bf16[1,4096,1024]{2,1,0:T(8,128)(2,1)} %w_first_in.1, bf16[1,1024,4096]{2,1,0:T(8,128)(2,1)} %w_second_in.1, ...), custom_call_target="tpu_custom_call" | custom-call | tf_op jit(solution)/shard_map/experts/pallas_call | solution.py:509
  219.1 2.3 %copy.49 = bf16[128,4096]{1,0:T(8,128)(2,1)} copy(bf16[128,4096]{1,0:T(8,128)(2,1)} %experts.1) | data formatting | bytes 2097152
  (43 shorter events, 0.2 us)
Async XLA Ops:
  6.5 1.2 copy-start
  6.5 11.2 %copy-start.12 = (s32[32]{0:T(128)S(1)}, s32[32]{0:T(128)}, u32[]{:S(2)}) copy-start(s32[32]{0:T(128)} %param.20) | copy-start | bytes 388
  6.5 11.3 %copy-start.13 = (s32[32]{0:T(128)S(1)}, s32[32]{0:T(128)}, u32[]{:S(2)}) copy-start(s32[32]{0:T(128)} %param.19) | copy-start | bytes 388
  6.5 44.7 %copy-start.5 = (bf16[4096,128]{1,0:T(8,128)(2,1)S(1)}, bf16[4096,128]{1,0:T(8,128)(2,1)}, u32[]{:S(2)}) copy-start(bf16[4096,128]{1,0:T(8,128)(2,1)} %param.22) | copy-start | bytes 3145732
  6.5 45.6 %copy-start.8 = (s32[16384]{0:T(1024)S(1)}, s32[16384]{0:T(1024)}, u32[]{:S(2)}) copy-start(s32[16384]{0:T(1024)} %param.18) | copy-start | bytes 196612
  6.5 46.3 %copy-start.6 = (bf16[128,4096]{1,0:T(8,128)(2,1)S(1)}, bf16[128,4096]{1,0:T(8,128)(2,1)}, u32[]{:S(2)}) copy-start(bf16[128,4096]{1,0:T(8,128)(2,1)} %param.16) | copy-start | bytes 3145732
  9.0 51.3 %all-to-all-start.2 = ((bf16[128,32,128]{2,0,1:T(8,128)(2,1)}), bf16[128,32,128]{2,0,1:T(8,128)(2,1)}, u32[]{:S(2)}, u32[]{:S(2)}) async-start(bf16[128,32,128]{2,0,1:T(8,128)(2,1)} %copy_bitcast_fusion), calls=%async_computation.2 | async-start | bytes 2097152 | tf_op jit(solution)/shard_map/all_to_all | solution.py:608
  17.7 109.0 %all-gather.2.cloned.1.call-start = ((), (), s32[]{:S(2)}) async-start(), calls=%async_computation.3 | async-start | bytes 2113536 | tf_op jit(solution)/shard_map/all_gather | solution.py:604
  51.2 4.2 %copy-start.11 = (s32[32,1]{0,1:T(1,128)S(1)}, s32[32,1]{0,1:T(1,128)}, u32[]{:S(2)}) copy-start(s32[32,1]{0,1:T(1,128)} %param.27) | copy-start | bytes 388
  51.2 4.3 %copy-start.10 = (s32[32,1,2]{0,2,1:T(2,128)S(1)}, s32[32,1,2]{0,2,1:T(2,128)}, u32[]{:S(2)}) copy-start(s32[32,1,2]{0,2,1:T(2,128)} %param.26) | copy-start | bytes 772
  52.1 1.9 copy-start.7
  60.4 15.0 %copy-start.9 = (bf16[4096,32]{0,1:T(8,128)(2,1)S(1)}, bf16[4096,32]{0,1:T(8,128)(2,1)}, u32[]{:S(2)}) copy-start(bf16[4096,32]{0,1:T(8,128)(2,1)} %param.23) | copy-start | bytes 786436
  60.4 22.0 %all-to-all-start.1 = ((bf16[128,32,128]{2,0,1:T(8,128)(2,1)}), bf16[128,32,128]{2,0,1:T(8,128)(2,1)}, u32[]{:S(2)}, u32[]{:S(2)}) async-start(bf16[128,32,128]{2,0,1:T(8,128)(2,1)} %copy_bitcast_fusion.1), calls=%async_computation.1 | async-start | bytes 2097152 | tf_op jit(solution)/shard_map/all_to_all | solution.py:607
  69.7 24.0 %collective-permute-start.2 = (bf16[1024,128]{1,0:T(8,128)(2,1)}, bf16[1024,128]{1,0:T(8,128)(2,1)S(1)}, u32[]{:S(2)}, u32[]{:S(2)}) collective-permute-start(bf16[1024,128]{1,0:T(8,128)(2,1)} %bitcast.9), channel_id=1, source_target_pairs={{0,1},{1,2},{2,3},{4,5},{5,6},{6,7},{8,9},{9,10},{10,11},{12,13},{... | collective-permute-start | bytes 786440 | tf_op jit(solution)/shard_map/ppermute | solution.py:24
  73.2 20.4 %collective-permute-start.3 = (bf16[1024,128]{1,0:T(8,128)(2,1)}, bf16[1024,128]{1,0:T(8,128)(2,1)}, u32[]{:S(2)}, u32[]{:S(2)}) collective-permute-start(bf16[1024,128]{1,0:T(8,128)(2,1)} %bitcast.11), channel_id=1, source_target_pairs={{1,0},{2,1},{3,2},{5,4},{6,5},{7,6},{9,8},{10,9},{11,10},{13,12},{... | collective-permute-start | bytes 786440 | tf_op jit(solution)/shard_map/ppermute | solution.py:26
  82.4 22.2 %all-to-all-start = ((bf16[128,32,128]{2,0,1:T(8,128)(2,1)}), bf16[128,32,128]{2,0,1:T(8,128)(2,1)}, u32[]{:S(2)}, u32[]{:S(2)}) async-start(bf16[128,32,128]{2,0,1:T(8,128)(2,1)} %copy_bitcast_fusion.2), calls=%async_computation | async-start | bytes 2097152 | tf_op jit(solution)/shard_map/all_to_all | solution.py:606
  88.1 9.7 %collective-permute-start = (bf16[1024,128]{1,0:T(8,128)(2,1)S(1)}, bf16[1024,128]{1,0:T(8,128)(2,1)S(1)}, u32[]{:S(2)}, u32[]{:S(2)}) collective-permute-start(bf16[1024,128]{1,0:T(8,128)(2,1)S(1)} %bitcast.57), channel_id=1, source_target_pairs={{0,1},{1,2},{2,3},{4,5},{5,6},{6,7},{8,9},{9,10},{10,11},{12,13},{... | collective-permute-start | bytes 786440 | tf_op jit(solution)/shard_map/ppermute | solution.py:24
  92.3 9.6 %collective-permute-start.1 = (bf16[1024,128]{1,0:T(8,128)(2,1)S(1)}, bf16[1024,128]{1,0:T(8,128)(2,1)S(1)}, u32[]{:S(2)}, u32[]{:S(2)}) collective-permute-start(bf16[1024,128]{1,0:T(8,128)(2,1)S(1)} %bitcast.56), channel_id=1, source_target_pairs={{1,0},{2,1},{3,2},{5,4},{6,5},{7,6},{9,8},{10,9},{11,10},{13,12},{... | collective-permute-start | bytes 786440 | tf_op jit(solution)/shard_map/ppermute | solution.py:26
  104.6 1.4 copy-start.1
  106.0 1.5 copy-start.2
  107.6 1.2 copy-start.4
  125.7 1.0 copy-start.3
Sparse Core Ops, SparseCore 0:
  52.3 71.3 all-gather.1

commit v3 on v2

--- a/solution.py
+++ b/solution.py
@@ -11,23 +11,6 @@
 
 
 EPS = 1e-06
-
-
-def with_halo(cells, sides, width):
-    for axis, dim in sides:
-        count = lax.axis_size(axis)
-        ends = count - 1
-        head = lax.slice_in_dim(cells, 0, width, axis=dim)
-        tail = lax.slice_in_dim(cells, cells.shape[dim] - width, cells.shape[dim], axis=dim)
-        cells = jnp.concatenate(
-            [
-                lax.ppermute(tail, axis, [(i, (i + 1) % count) for i in range(ends)]),
-                cells,
-                lax.ppermute(head, axis, [((i + 1) % count, i) for i in range(ends)]),
-            ],
-            axis=dim,
-        )
-    return cells
 
 
 Q_ROWS = 256
@@ -66,28 +49,10 @@
         with_parts(number)
 
 
-def local_attention(head_query, keys, values, sample_id, exp_index):
+def local_attention(spans, head_query, query_tags, keys, key_tags, values):
     group, head_width = head_query.shape
     extent = keys.shape[0]
     blocks = group // Q_ROWS
-    first_token = exp_index * group
-    images = jnp.arange(head_width, dtype=jnp.int32)[None, :]
-    query_ids = lax.dynamic_slice_in_dim(sample_id, first_token, group, 0)
-    id_padded = jnp.pad(sample_id, (MOST, MOST), constant_values=-1)
-    key_ids = lax.dynamic_slice_in_dim(id_padded, first_token, extent, 0)
-    query_tags = (query_ids[:, None] == images).astype(jnp.bfloat16)
-    key_tags = jnp.where(key_ids[:, None] == images, 0.0, -FAR).astype(jnp.bfloat16)
-    begins = jnp.sum(
-        (sample_id[None, :] < jnp.arange(33, dtype=jnp.int32)[:, None]).astype(jnp.int32), axis=1
-    )
-    by_block = query_ids.reshape(blocks, Q_ROWS)
-    shown = jnp.arange(33, dtype=jnp.int32)[None, :]
-    low = jnp.sum(jnp.where(by_block[:, :1] == shown, begins[None, :], 0), axis=1)
-    high = jnp.sum(jnp.where(by_block[:, -1:] + 1 == shown, begins[None, :], 0), axis=1)
-    low = (low - first_token + MOST) // 128 * 128
-    high = high - first_token + MOST
-    parts = jnp.maximum((high - low + Q_ROWS - 1) // Q_ROWS, 2)
-    spans = jnp.stack([low, parts]).astype(jnp.int32)
     whole = lambda step, spans: (0, 0)
     part = lambda step, spans: (step, 0)
     return pl.pallas_call(
@@ -105,7 +70,7 @@
             out_specs=pl.BlockSpec((Q_ROWS, head_width), part),
         ),
         out_shape=jax.ShapeDtypeStruct((group, head_width), jnp.bfloat16),
-        compiler_params=pltpu.CompilerParams(vmem_limit_bytes=40 * 2**20),
+        compiler_params=pltpu.CompilerParams(vmem_limit_bytes=60 * 2**20),
         name="attention",
     )(spans, head_query, query_tags, keys, key_tags, values)
 
@@ -153,19 +118,320 @@
     return pl.ds(pl.multiple_of(number * size, size), size)
 
 
+def exchange_kernel(
+    query_in,
+    key_in,
+    value_in,
+    weight_in,
+    condition_ref,
+    ids_ref,
+    query_out,
+    key_out,
+    value_out,
+    query_tags_out,
+    key_tags_out,
+    modulation_out,
+    spans_out,
+    conditions,
+    weight,
+    own_modulation,
+    query_tags,
+    key_tags,
+    local_sem,
+    c_send,
+    c_recv,
+    p_send,
+    p_recv,
+    h_send,
+    h_recv,
+    m_send,
+    m_recv,
+):
+    seq_index = lax.axis_index("seq")
+    exp_index = lax.axis_index("exp")
+    tokens = query_in.shape[0]
+    group, head_width = query_out.shape
+    at_y = seq_index // 8
+    at_x = seq_index // 2 % 4
+    core = seq_index % 2
+    f32 = jnp.float32
+    bf16 = jnp.bfloat16
+
+    greet(seq_index, exp_index, [(exp_index + step) % 4 for step in (1, 2, 3)])
+
+    def copy_to(source, target, send, recv, peer, other):
+        return pltpu.make_async_remote_copy(
+            src_ref=source,
+            dst_ref=target,
+            send_sem=send,
+            recv_sem=recv,
+            device_id=(peer, other),
+            device_id_type=MESH,
+        )
+
+    load_weight = pltpu.make_async_copy(weight_in, weight, local_sem.at[0])
+    load_weight.start()
+
+    def condition_copy(offset):
+        return copy_to(
+            condition_ref,
+            conditions.at[seq_index],
+            c_send.at[offset],
+            c_recv.at[offset],
+            shifted(seq_index, offset, 1),
+            exp_index,
+        )
+
+    for_offsets(lambda offset: condition_copy(offset).start())
+    conditions[seq_index] = condition_ref[...]
+
+    arrays = ((key_in, key_out, MOST), (value_in, value_out, MOST), (query_in, query_out, 0))
+
+    def head_copy(which, offset):
+        source, target, before = arrays[which]
+        peer = shifted(seq_index, offset, 1)
+        return copy_to(
+            source.at[:, rows_of(peer, head_width)],
+            target.at[pl.ds(pl.multiple_of(before + seq_index * tokens, tokens), tokens)],
+            p_send.at[which, offset],
+            p_recv.at[which, offset],
+            peer,
+            exp_index,
+        )
+
+    def own_head_copy(which):
+        source, target, before = arrays[which]
+        return pltpu.make_async_copy(
+            source.at[:, rows_of(seq_index, head_width)],
+            target.at[pl.ds(pl.multiple_of(before + seq_index * tokens, tokens), tokens)],
+            local_sem.at[1 + which],
+        )
+
+    def send_heads(which):
+        own_head_copy(which).start()
+        for_offsets(lambda offset: head_copy(which, offset).start())
+
+    def wait_heads(which):
+        own_head_copy(which).wait()
+        for_offsets(lambda offset: head_copy(which, offset).wait_recv())
+
+    def halo_copies(which):
+        target = arrays[which][1]
+        return (
+            copy_to(
+                target.at[pl.ds(MOST, MOST)],
+                target.at[pl.ds(MOST + group, MOST)],
+                h_send.at[which, 0],
+                h_recv.at[which, 0],
+                seq_index,
+                (exp_index + 3) % 4,
+            ),
+            copy_to(
+                target.at[pl.ds(group, MOST)],
+                target.at[pl.ds(0, MOST)],
+                h_send.at[which, 1],
+                h_recv.at[which, 1],
+                seq_index,
+                (exp_index + 1) % 4,
+            ),
+        )
+
+    slot = ((core * 4 + exp_index) * 4 + at_y) * 4 + at_x
+
+    def modulation_copies(phase):
+        if phase == 0:
+            source, target = own_modulation, modulation_out.at[slot]
+            places = [((at_y * 4 + (at_x + d) % 4) * 2 + core, exp_index) for d in (1, 2, 3)]
+        elif phase == 1:
+            source = modulation_out.at[rows_of(slot // 4, 4)]
+            target = source
+            places = [((((at_y + d) % 4) * 4 + at_x) * 2 + core, exp_index) for d in (1, 2, 3)]
+        elif phase == 2:
+            source = modulation_out.at[rows_of(slot // 16, 16)]
+            target = source
+            places = [(seq_index, (exp_index + d) % 4) for d in (1, 2, 3)]
+        else:
+            source = modulation_out.at[rows_of(core, 64)]
+            target = source
+            places = [(at_y * 8 + at_x * 2 + 1 - core, exp_index)]
+        return [
+            copy_to(source, target, m_send.at[phase, i], m_recv.at[phase, i], peer, other)
+            for i, (peer, other) in enumerate(places)
+        ]
+
+    def send_modulation(phase):
+        for copy in modulation_copies(phase):
+            copy.start()
+
+    def wait_modulation(phase):
+        for copy in modulation_copies(phase):
+            copy.wait_recv()
+
+    send_heads(0)
+
+    for_offsets(lambda offset: condition_copy(offset).wait_recv())
+    load_weight.wait()
+    condition = jnp.concatenate([conditions[place] for place in range(PLANE)], axis=1)
+    own_modulation[...] = jnp.dot(condition, weight[...], preferred_element_type=f32).astype(bf16)
+    keep = pltpu.make_async_copy(own_modulation, modulation_out.at[slot], local_sem.at[4])
+    keep.start()
+    send_modulation(0)
+    send_heads(1)
+
+    ids = ids_ref[...]
+    lane = lax.broadcasted_iota(jnp.int32, (1, head_width), 1)
+
+    def total(mask):
+        return jnp.sum(
+            jnp.sum(jnp.where(mask, 1.0, 0.0), axis=0, keepdims=True), axis=1, keepdims=True
+        )
+
+    begins = jnp.zeros((1, head_width), f32)
+    ends = jnp.zeros((1, head_width), f32)
+    for image in range(32):
+        begins = begins + jnp.where(lane == image, total(ids < image), 0.0)
+        ends = ends + jnp.where(lane == image, total(ids <= image), 0.0)
+    begins = begins.astype(jnp.int32)
+    ends = ends.astype(jnp.int32)
+    first_token = exp_index * group
+
+    def tag_rows(step, carry):
+        rows = rows_of(step, Q_ROWS)
+        shape = (Q_ROWS, head_width)
+        place = lax.broadcasted_iota(jnp.int32, shape, 0) + (first_token - MOST + step * Q_ROWS)
+        same = (place >= begins) & (place < ends)
+        key_tags[rows, :] = jnp.where(same, 0.0, -FAR).astype(bf16)
+        return carry
+
+    def query_tag_rows(step, carry):
+        rows = rows_of(step, Q_ROWS)
+        shape = (Q_ROWS, head_width)
+        place = lax.broadcasted_iota(jnp.int32, shape, 0) + (first_token + step * Q_ROWS)
+        same = (place >= begins) & (place < ends)
+        query_tags[rows, :] = jnp.where(same, 1.0, 0.0).astype(bf16)
+        return carry
+
+    lax.fori_loop(0, key_tags.shape[0] // Q_ROWS, tag_rows, 0)
+    lax.fori_loop(0, group // Q_ROWS, query_tag_rows, 0)
+    keep_key_tags = pltpu.make_async_copy(key_tags, key_tags_out, local_sem.at[5])
+    keep_key_tags.start()
+    keep_query_tags = pltpu.make_async_copy(query_tags, query_tags_out, local_sem.at[6])
+    keep_query_tags.start()
+
+    low = jnp.zeros((1, head_width), f32)
+    high = jnp.zeros((1, head_width), f32)
+    for block in range(group // Q_ROWS):
+        line = exp_index * (group // 128) + block * (Q_ROWS // 128)
+        first = ids_ref[pl.ds(line, 1), 0:1]
+        last = ids_ref[pl.ds(line + Q_ROWS // 128 - 1, 1), 127:128]
+        low = low + jnp.where(lane == block, total(ids < first), 0.0)
+        high = high + jnp.where(lane == block, total(ids <= last), 0.0)
+    low = (low.astype(jnp.int32) - first_token + MOST) & ~127
+    high = high.astype(jnp.int32) - first_token + MOST
+    parts = jnp.maximum((high - low + Q_ROWS - 1) >> 8, 2)
+    spans_out[...] = jnp.where(
+        lax.broadcasted_iota(jnp.int32, spans_out.shape, 0) == 0, low, parts
+    )
+
+    keep.wait()
+    wait_modulation(0)
+    send_modulation(1)
+    wait_modulation(1)
+    send_modulation(2)
+    wait_heads(0)
+    for copy in halo_copies(0):
+        copy.start()
+    send_heads(2)
+    wait_modulation(2)
+    send_modulation(3)
+    wait_heads(1)
+    for copy in halo_copies(1):
+        copy.start()
+    wait_heads(2)
+    wait_modulation(3)
+    keep_key_tags.wait()
+    keep_query_tags.wait()
+    for which in range(2):
+        for copy in halo_copies(which):
+            copy.wait_recv()
+    for_offsets(lambda offset: condition_copy(offset).wait_send())
+    for which in range(3):
+        for_offsets(lambda offset: head_copy(which, offset).wait_send())
+    for which in range(2):
+        for copy in halo_copies(which):
+            copy.wait_send()
+    for phase in range(4):
+        for copy in modulation_copies(phase):
+            copy.wait_send()
+
+
+def exchange(query_input, key_input, value_input, mod_weight, cond_columns, sample_id):
+    tokens, width = query_input.shape
+    head_width = width // PLANE
+    group = tokens * PLANE
+    extent = group + 2 * MOST
+    bf16 = jnp.bfloat16
+    samples = cond_columns.shape[0]
+    anywhere = pl.BlockSpec(memory_space=pl.ANY)
+    inside = pl.BlockSpec(memory_space=pltpu.VMEM)
+    dma = pltpu.SemaphoreType.DMA
+    return pl.pallas_call(
+        exchange_kernel,
+        out_shape=(
+            jax.ShapeDtypeStruct((group, head_width), bf16),
+            jax.ShapeDtypeStruct((extent, head_width), bf16),
+            jax.ShapeDtypeStruct((extent, head_width), bf16),
+            jax.ShapeDtypeStruct((group, head_width), bf16),
+            jax.ShapeDtypeStruct((extent, head_width), bf16),
+            jax.ShapeDtypeStruct((4 * PLANE, samples, mod_weight.shape[1]), bf16),
+            jax.ShapeDtypeStruct((8, head_width), jnp.int32),
+        ),
+        in_specs=[anywhere] * 4 + [inside] * 2,
+        out_specs=(anywhere,) * 6 + (inside,),
+        scratch_shapes=[
+            pltpu.VMEM((PLANE, samples, head_width), bf16),
+            pltpu.VMEM(mod_weight.shape, bf16),
+            pltpu.VMEM((samples, mod_weight.shape[1]), bf16),
+            pltpu.VMEM((group, head_width), bf16),
+            pltpu.VMEM((extent, head_width), bf16),
+            dma((7,)),
+            dma((PLANE,)),
+            dma((PLANE,)),
+            dma((3, PLANE)),
+            dma((3, PLANE)),
+            dma((2, 2)),
+            dma((2, 2)),
+            dma((4, 3)),
+            dma((4, 3)),
+        ],
+        compiler_params=pltpu.CompilerParams(
+            collective_id=0, has_side_effects=True, vmem_limit_bytes=60 * 2**20
+        ),
+        name="exchange",
+    )(
+        query_input,
+        key_input,
+        value_input,
+        mod_weight,
+        cond_columns,
+        sample_id.reshape(-1, head_width),
+    )
+
+
 def experts_kernel(
     attended_ref,
     stream_in,
     modulation_in,
     w_first_in,
     w_second_in,
-    selector_ref,
+    tags_in,
     target_ref,
     placement_ref,
     router_ref,
     out_ref,
     stream_ref,
     modulation_ref,
+    selector_ref,
     w_first,
     w_second,
     attended,
@@ -190,6 +456,7 @@
     own_total,
     homeward,
     back,
+    router_twice,
     local_sem,
     a_send,
     a_recv,
@@ -252,6 +519,10 @@
     load_mod.start()
     load_stream = pltpu.make_async_copy(stream_in, stream_ref, local_sem.at[2])
     load_stream.start()
+    load_tags = pltpu.make_async_copy(
+        tags_in.at[rows_of(seq_index, tokens)], selector_ref, local_sem.at[5]
+    )
+    load_tags.start()
     load_first = pltpu.make_async_copy(w_first_in.at[0], w_first, local_sem.at[3])
     load_first.start()
     load_second = pltpu.make_async_copy(w_second_in.at[0], w_second, local_sem.at[4])
@@ -270,21 +541,24 @@
     load_mod.wait()
     load_stream.wait()
 
+    load_tags.wait()
+    samples = modulation_ref.shape[1]
+
     def spread_mod(step, carry):
-        columns = rows_of(step, 512)
-        whole = modulation_ref[:, columns]
-        first = whole.astype(bf16)
-        rest = whole - first.astype(f32)
-        second = rest.astype(bf16)
-        third = (rest - second.astype(f32)).astype(bf16)
-        token_mod[:, columns] = jnp.dot(
-            selector_ref[...],
-            jnp.concatenate([first, second, third], axis=0),
-            preferred_element_type=f32,
+        base = (step % 2 * 16 + step // 8) * 4 + step // 2 % 4
+        whole = jnp.concatenate([modulation_ref[base + 16 * part] for part in range(4)], axis=1)
+        token_mod[:, rows_of(step, 512)] = jnp.dot(
+            selector_ref[:, :samples], whole, preferred_element_type=f32
         )
         return carry
 
     lax.fori_loop(0, 4 * width // 512, spread_mod, 0)
+
+    double = lax.broadcasted_iota(jnp.int32, (SLOT_ROWS, samples), 0) >> 1
+    twice = jnp.where(
+        double == lax.broadcasted_iota(jnp.int32, (SLOT_ROWS, samples), 1), 1.0, 0.0
+    ).astype(bf16)
+    router_twice[...] = jnp.dot(twice, router_ref[...], preferred_element_type=f32).astype(bf16)
 
     own_attended.wait()
     for_offsets(lambda offset: attended_copy(offset).wait_recv())
@@ -326,7 +600,9 @@
         for_offsets(lambda offset: dispatch_copy(half, offset).start())
         landed[half, rows_of(seq_index, 16), :] = outgoing[half, rows_of(seq_index, 16), :]
 
-    logits = jnp.dot(normed[...], router_ref[...], preferred_element_type=f32)
+    logits = lax.dot_general(
+        normed[...], router_twice[...], (((1,), (1,)), ((), ())), preferred_element_type=f32
+    )
     weighted = placement_ref[...] / (1.0 + jnp.exp(-logits))
     weight_first = weighted.astype(bf16)
     weight_rest = weighted - weight_first.astype(f32)
@@ -496,7 +772,7 @@
 
 
 def feed_forward(
-    attended_head, stream, modulation, expert_in, expert_out, selector, target, placement, router
+    attended_head, stream, modulation, expert_in, expert_out, query_tags, target, placement, router
 ):
     tokens, width = stream.shape
     bf16 = jnp.bfloat16
@@ -509,11 +785,12 @@
     return pl.pallas_call(
         experts_kernel,
         out_shape=jax.ShapeDtypeStruct((tokens, width), bf16),
-        in_specs=[anywhere] * 5 + [inside] * 4,
+        in_specs=[anywhere] * 6 + [inside] * 3,
         out_specs=inside,
         scratch_shapes=[
             pltpu.VMEM((tokens, width), bf16),
-            pltpu.VMEM(modulation.shape, f32),
+            pltpu.VMEM(modulation.shape, bf16),
+            pltpu.VMEM((tokens, width // PLANE), bf16),
             pltpu.VMEM((width, part), bf16),
             pltpu.VMEM((part, width), bf16),
             pltpu.VMEM((PLANE, tokens, width // PLANE), bf16),
@@ -538,7 +815,8 @@
             pltpu.VMEM((2, SLOT_ROWS, HALF), f32),
             pltpu.VMEM((2, block, TILE), bf16),
             pltpu.VMEM((2, block, TILE), bf16),
-            dma((5,)),
+            pltpu.VMEM((SLOT_ROWS, width), bf16),
+            dma((6,)),
             dma((PLANE,)),
             dma((PLANE,)),
             dma((2, PLANE)),
@@ -560,7 +838,7 @@
         modulation,
         expert_in,
         expert_out,
-        selector,
+        query_tags,
         target,
         placement,
         router,
@@ -583,12 +861,8 @@
     picked,
     counts,
 ):
-    seq_count = lax.axis_size("seq")
     seq_index = lax.axis_index("seq")
-    exp_index = lax.axis_index("exp")
     tok_local, width = stream.shape
-    group = tok_local * seq_count
-    owner_block = exp_index * seq_count + seq_index
     column_count = class_table.shape[1]
     half_width = width // 2
     column = seq_index * column_count + jnp.arange(column_count, dtype=jnp.int32)
@@ -599,27 +873,10 @@
     embedded = jnp.where(first_half[None, :], jnp.cos(angles), jnp.sin(angles))
     table_rows = jnp.take(class_table, class_id, axis=0).astype(jnp.float32)
     cond_columns = jax.nn.silu(embedded + table_rows).astype(jnp.bfloat16)
-    condition = lax.all_gather(cond_columns, "seq", axis=1, tiled=True)
-    local_mod = jnp.dot(condition, mod_weight, preferred_element_type=jnp.float32)
-    modulation = lax.all_gather(local_mod, ("seq", "exp"), axis=1, tiled=True)
-    head_query, head_key, head_value = (
-        lax.all_to_all(query_input, "seq", split_axis=1, concat_axis=0, tiled=True),
-        lax.all_to_all(key_input, "seq", split_axis=1, concat_axis=0, tiled=True),
-        lax.all_to_all(value_input, "seq", split_axis=1, concat_axis=0, tiled=True),
-    )
-    sides = (("exp", 0),)
-    attended_head = local_attention(
-        head_query,
-        with_halo(head_key, sides, MOST),
-        with_halo(head_value, sides, MOST),
-        sample_id,
-        exp_index,
-    )
-    own_ids = lax.dynamic_slice_in_dim(sample_id, owner_block * tok_local, tok_local, 0)
-    samples = modulation.shape[0]
-    selector = (
-        own_ids[:, None] == jnp.arange(3 * samples, dtype=jnp.int32)[None, :] % samples
-    ).astype(jnp.bfloat16)
+    head_query, keys, values, query_tags, key_tags, modulation, spans = exchange(
+        query_input, key_input, value_input, mod_weight, cond_columns, sample_id
+    )
+    attended_head = local_attention(spans, head_query, query_tags, keys, key_tags, values)
     slots = picked[:, 0, :]
     expert_count, slot_total = slots.shape
     live = jnp.arange(slot_total, dtype=jnp.int32)[None, :] < counts[:, 0][:, None]
@@ -635,10 +892,10 @@
         modulation,
         expert_in,
         expert_out,
-        selector,
+        query_tags,
         target,
         placement,
-        jnp.repeat(router_weight, slot_total, axis=1),
+        router_weight.T,
     )
 
 

time: 229 us -> 178 us (0.78)
  Pallas kernels: 109 us -> 170 us
  blocking collectives: 31.6 us -> 0 us
  starting transfers between devices: 28.3 us -> 0 us
  local copies, waits for them, and re-layouts: 22.2 us -> 4.32 us
  between operations: 13.7 us -> 0.07 us
  other arithmetic: 13.1 us -> 3.59 us
  waiting for transfers between devices: 9.08 us -> 0 us
    pallas_call x0 -> x1, Pallas kernels: none -> 62.8 us  [exchange(): pl.pallas_call(exchange_kernel, out_shape=(jax.ShapeDtypeStruct((group, h...]
    all_gather x1 -> x0, blocking collectives: 31.6 us -> none  [on_device(): condition = lax.all_gather(cond_columns, 'seq', axis=1, tiled=True)]
    all_to_all x3 -> x0, starting transfers between devices: 18 us -> none  [the longest x1 8.64 us: on_device(): lax.all_to_all(value_input, 'seq', split_axis=1, concat_axis=0, tiled=True)]
    ppermute x4 -> x0, starting transfers between devices: 10.3 us -> none  [the longest x2 7.76 us: with_halo(): lax.ppermute(tail, axis, [(i, (i + 1) % count) for i in range(ends)])]
    convert_element_type x3 -> x0, other arithmetic: 6.24 us -> none  [the longest x1 2.83 us: local_attention(): jnp.where(key_ids[:, None] == images, 0.0, -FAR).astype(jnp.bfloat16)]
    unnamed x30 -> x8, local copies, waits for them, and re-layouts: 8.76 us -> 2.62 us
    ppermute x4 -> x0, waiting for transfers between devices: 5.72 us -> none  [the longest x2 4.17 us: with_halo(): lax.ppermute(head, axis, [((i + 1) % count, i) for i in range(ends)])]
    pallas_call x1, Pallas kernels: 92.5 us -> 87.3 us  [feed_forward(): pl.pallas_call(experts_kernel, out_shape=jax.ShapeDtypeStruct((tokens, wi...]
  transfers between devices with their start and end apart: 8 -> 0, of which waited for: 4 -> 0; matrix products, arithmetic and copies ran while one was open for 11% -> 0% of each run, Pallas kernels for 7% -> 0%
where the time goes in v3:
time: 178 us
  Pallas kernels  170 us (96%)
  local copies, waits for them, and re-layouts  4.32 us (2%)
  other arithmetic  3.59 us (2%)
    pallas_call x1, Pallas kernels, feed_forward(): pl.pallas_call(experts_kernel, out_shape=jax.ShapeDtypeStruct((tokens, wi...  87.3 us
    pallas_call x1, Pallas kernels, exchange(): pl.pallas_call(exchange_kernel, out_shape=(jax.ShapeDtypeStruct((group, h...  62.8 us
    pallas_call x1, Pallas kernels, local_attention(): pl.pallas_call(attention_kernel, grid_spec=pltpu.PrefetchScalarGridSpec(n...  19.7 us

profile of v3, /device:TPU:1, one launch (start us, length us, event | category | flops | bytes accessed | tf_op | source)
XLA Modules:
  0.0 177.8 jit_solution(4298145871726403181)
XLA Ops:
  0.0 0.0 copy-start
  0.0 0.7 compare_select_fusion
  0.7 0.2 copy-done
  1.0 0.6 gather_fusion
  1.6 0.7 compare_and_fusion
  2.2 0.7 convert_element_type.19
  2.9 0.8 multiply_convert_fusion.condition_ref
  3.6 62.8 %exchange.1 = (bf16[4096,128]{1,0:T(8,128)(2,1)}, bf16[6144,128]{1,0:T(8,128)(2,1)}, bf16[6144,128]{1,0:T(8,128)(2,1)}, bf16[4096,128]{1,0:T(8,128)(2,1)}, bf16[...) custom-call(bf16[128,4096]{1,0:T(8,128)(2,1)} %query_in.1, bf16[128,4096]{1,0:T(8,128)(2,1)} %key_in.1, ...), custom_call_target="tpu_custom_call" | custom-call | tf_op jit(solution)/shard_map/exchange/pallas_call | solution.py:378
  66.5 0.0 copy-start.2
  66.5 0.0 copy-start.1
  66.5 19.7 %attention.1.attended_ref = bf16[4096,128]{1,0:T(8,128)(2,1)} custom-call(s32[8,128]{1,0:T(8,128)} %get-tuple-element.12.spans, bf16[4096,128]{1,0:T(8,128)(2,1)} %get-tuple-element.13.q_ref, bf16[4096,128]{1,0:T(8,128)(2,1)} %get-tuple-element.14.fq_ref.tags_in, bf16[6144,128]{1,0:T(8,128)(2,1)} %get-tuple-element.15.k_ref, ...), custom_call_target="tpu_custom_call" | custom-call | tf_op jit(solution)/shard_map/attention/pallas_call | solution.py:58
  86.2 0.0 copy-done.2
  86.2 0.1 iota_compare_fusion.1
  86.3 0.0 copy-done.1
  86.3 0.1 copy.17
  86.4 0.1 add_select_fusion
  86.5 0.8 select_n.50.target_ref
  87.3 0.1 lt.51
  87.4 0.1 copy.18
  87.5 0.1 squeeze.3
  87.6 0.6 fusion.placement_ref
  88.2 87.3 %experts.1 = bf16[128,4096]{1,0:T(8,128)(2,1)} custom-call(bf16[4096,128]{1,0:T(8,128)(2,1)} %attention.1.attended_ref, bf16[128,4096]{1,0:T(8,128)(2,1)} %stream_in.1, bf16[128,32,128]{2,1,0:T(8,128)(2,1)} %get-tuple-element.18.modulation_in, bf16[1,4096,1024]{2,1,0:T(8,128)(2,1)} %w_first_in.1, bf16[1,1024,4096]{2,1,0:T(8,128)(2,1)} %w_second_in.1, ...), custom_call_target="tpu_custom_call" | custom-call | tf_op jit(solution)/shard_map/experts/pallas_call | solution.py:785
  175.5 2.3 %copy.21 = bf16[128,4096]{1,0:T(8,128)(2,1)} copy(bf16[128,4096]{1,0:T(8,128)(2,1)} %experts.1) | data formatting | bytes 2097152
  (5 shorter events, 0.0 us)
Async XLA Ops:
  0.0 1.0 copy-start
  66.5 19.7 %copy-start.2 = (s32[32,1]{0,1:T(1,128)S(1)}, s32[32,1]{0,1:T(1,128)}, u32[]{:S(2)}) copy-start(s32[32,1]{0,1:T(1,128)} %param.27) | copy-start | bytes 388
  66.5 19.8 %copy-start.1 = (s32[32,1,2]{0,2,1:T(2,128)S(1)}, s32[32,1,2]{0,2,1:T(2,128)}, u32[]{:S(2)}) copy-start(s32[32,1,2]{0,2,1:T(2,128)} %param.26) | copy-start | bytes 772

commit v4 on v3

--- a/solution.py
+++ b/solution.py
@@ -83,35 +83,25 @@
 SLOT_ROWS = 64
 
 
-def shifted(place, offset, sign):
-    high = (place // 8 + sign * (offset // 8) + 4) % 4
-    middle = (place // 2 % 4 + sign * (offset // 2 % 4) + 4) % 4
-    return high * 8 + middle * 2 + (place + offset) % 2
-
-
-def for_offsets(body):
-    def step(index, carry):
-        body((index * 13) % PLANE)
-        return carry
-
-    lax.fori_loop(1, PLANE, step, 0)
+OFFSETS = sorted(range(1, PLANE), key=lambda offset: (offset * 13) % PLANE)
 
 
 def greet(seq_index, exp_index, ring):
     barrier = pltpu.get_barrier_semaphore()
-
-    def hello(offset):
+    for offset in OFFSETS:
         pl.semaphore_signal(
             barrier,
             inc=1,
-            device_id=(shifted(seq_index, offset, 1), exp_index),
+            device_id=(seq_index ^ offset, exp_index),
             device_id_type=MESH,
         )
-
-    for_offsets(hello)
     for other in ring:
         pl.semaphore_signal(barrier, inc=1, device_id=(seq_index, other), device_id_type=MESH)
     pl.semaphore_wait(barrier, PLANE - 1 + len(ring))
+
+
+def wait_for(part, semaphore):
+    pltpu.make_async_copy(part, part, semaphore).wait()
 
 
 def rows_of(number, size):
@@ -123,7 +113,9 @@
     key_in,
     value_in,
     weight_in,
-    condition_ref,
+    class_table_ref,
+    class_id_ref,
+    timestep_ref,
     ids_ref,
     query_out,
     key_out,
@@ -132,14 +124,14 @@
     key_tags_out,
     modulation_out,
     spans_out,
+    own_condition,
     conditions,
     weight,
     own_modulation,
     query_tags,
     key_tags,
     local_sem,
-    c_send,
-    c_recv,
+    c_sem,
     p_send,
     p_recv,
     h_send,
@@ -169,51 +161,28 @@
             device_id_type=MESH,
         )
 
-    load_weight = pltpu.make_async_copy(weight_in, weight, local_sem.at[0])
-    load_weight.start()
-
-    def condition_copy(offset):
-        return copy_to(
-            condition_ref,
-            conditions.at[seq_index],
-            c_send.at[offset],
-            c_recv.at[offset],
-            shifted(seq_index, offset, 1),
-            exp_index,
-        )
-
-    for_offsets(lambda offset: condition_copy(offset).start())
-    conditions[seq_index] = condition_ref[...]
-
     arrays = ((key_in, key_out, MOST), (value_in, value_out, MOST), (query_in, query_out, 0))
 
-    def head_copy(which, offset):
+    def send_heads(which):
         source, target, before = arrays[which]
-        peer = shifted(seq_index, offset, 1)
-        return copy_to(
-            source.at[:, rows_of(peer, head_width)],
-            target.at[pl.ds(pl.multiple_of(before + seq_index * tokens, tokens), tokens)],
-            p_send.at[which, offset],
-            p_recv.at[which, offset],
-            peer,
-            exp_index,
-        )
-
-    def own_head_copy(which):
-        source, target, before = arrays[which]
-        return pltpu.make_async_copy(
-            source.at[:, rows_of(seq_index, head_width)],
-            target.at[pl.ds(pl.multiple_of(before + seq_index * tokens, tokens), tokens)],
-            local_sem.at[1 + which],
-        )
-
-    def send_heads(which):
-        own_head_copy(which).start()
-        for_offsets(lambda offset: head_copy(which, offset).start())
+        place = target.at[pl.ds(pl.multiple_of(before + seq_index * tokens, tokens), tokens)]
+        for offset in OFFSETS:
+            peer = seq_index ^ offset
+            copy_to(
+                source.at[:, rows_of(peer, head_width)],
+                place,
+                p_send.at[which],
+                p_recv.at[which],
+                peer,
+                exp_index,
+            ).start()
+        pltpu.make_async_copy(
+            source.at[:, rows_of(seq_index, head_width)], place, p_recv.at[which]
+        ).start()
 
     def wait_heads(which):
-        own_head_copy(which).wait()
-        for_offsets(lambda offset: head_copy(which, offset).wait_recv())
+        _, target, before = arrays[which]
+        wait_for(target.at[pl.ds(before, group)], p_recv.at[which])
 
     def halo_copies(which):
         target = arrays[which][1]
@@ -268,8 +237,45 @@
             copy.wait_recv()
 
     send_heads(0)
-
-    for_offsets(lambda offset: condition_copy(offset).wait_recv())
+    load_weight = pltpu.make_async_copy(weight_in, weight, local_sem.at[0])
+    load_weight.start()
+
+    samples = timestep_ref.shape[1]
+    diagonal = lax.broadcasted_iota(jnp.int32, (samples, samples), 0) == lax.broadcasted_iota(
+        jnp.int32, (samples, samples), 1
+    )
+
+    def upright(row):
+        return jnp.sum(jnp.where(diagonal, row.astype(f32), 0.0), axis=1, keepdims=True)
+
+    classes = class_table_ref.shape[0]
+    chosen_class = jnp.where(
+        lax.broadcasted_iota(jnp.int32, (samples, classes), 1).astype(f32)
+        == upright(class_id_ref[...]),
+        1.0,
+        0.0,
+    ).astype(bf16)
+    table_rows = jnp.dot(chosen_class, class_table_ref[...], preferred_element_type=f32)
+    half_columns = PLANE * head_width // 2
+    column = seq_index * head_width + lax.broadcasted_iota(jnp.int32, (1, head_width), 1)
+    freq_index = jnp.where(column < half_columns, column, column - half_columns).astype(f32)
+    frequency = jnp.exp(-math.log(10000.0) * freq_index / half_columns)
+    angles = upright(timestep_ref[...]) * frequency
+    embedded = jnp.where(column < half_columns, jnp.cos(angles), jnp.sin(angles))
+    value = embedded + table_rows
+    own_condition[...] = (value / (1.0 + jnp.exp(-value))).astype(bf16)
+
+    for offset in OFFSETS:
+        copy_to(
+            own_condition,
+            conditions.at[seq_index],
+            c_sem.at[0],
+            c_sem.at[1],
+            seq_index ^ offset,
+            exp_index,
+        ).start()
+    pltpu.make_async_copy(own_condition, conditions.at[seq_index], c_sem.at[1]).start()
+    wait_for(conditions, c_sem.at[1])
     load_weight.wait()
     condition = jnp.concatenate([conditions[place] for place in range(PLANE)], axis=1)
     own_modulation[...] = jnp.dot(condition, weight[...], preferred_element_type=f32).astype(bf16)
@@ -354,9 +360,9 @@
     for which in range(2):
         for copy in halo_copies(which):
             copy.wait_recv()
-    for_offsets(lambda offset: condition_copy(offset).wait_send())
+    wait_for(conditions.at[pl.ds(0, PLANE - 1)], c_sem.at[0])
     for which in range(3):
-        for_offsets(lambda offset: head_copy(which, offset).wait_send())
+        wait_for(query_out.at[pl.ds(0, group - tokens)], p_send.at[which])
     for which in range(2):
         for copy in halo_copies(which):
             copy.wait_send()
@@ -365,13 +371,15 @@
             copy.wait_send()
 
 
-def exchange(query_input, key_input, value_input, mod_weight, cond_columns, sample_id):
+def exchange(
+    query_input, key_input, value_input, mod_weight, class_table, class_id, timestep, sample_id
+):
     tokens, width = query_input.shape
     head_width = width // PLANE
     group = tokens * PLANE
     extent = group + 2 * MOST
     bf16 = jnp.bfloat16
-    samples = cond_columns.shape[0]
+    samples = class_id.shape[0]
     anywhere = pl.BlockSpec(memory_space=pl.ANY)
     inside = pl.BlockSpec(memory_space=pltpu.VMEM)
     dma = pltpu.SemaphoreType.DMA
@@ -386,19 +394,19 @@
             jax.ShapeDtypeStruct((4 * PLANE, samples, mod_weight.shape[1]), bf16),
             jax.ShapeDtypeStruct((8, head_width), jnp.int32),
         ),
-        in_specs=[anywhere] * 4 + [inside] * 2,
+        in_specs=[anywhere] * 4 + [inside] * 4,
         out_specs=(anywhere,) * 6 + (inside,),
         scratch_shapes=[
+            pltpu.VMEM((samples, head_width), bf16),
             pltpu.VMEM((PLANE, samples, head_width), bf16),
             pltpu.VMEM(mod_weight.shape, bf16),
             pltpu.VMEM((samples, mod_weight.shape[1]), bf16),
             pltpu.VMEM((group, head_width), bf16),
             pltpu.VMEM((extent, head_width), bf16),
             dma((7,)),
-            dma((PLANE,)),
-            dma((PLANE,)),
-            dma((3, PLANE)),
-            dma((3, PLANE)),
+            dma((2,)),
+            dma((3,)),
+            dma((3,)),
             dma((2, 2)),
             dma((2, 2)),
             dma((4, 3)),
@@ -413,7 +421,9 @@
         key_input,
         value_input,
         mod_weight,
-        cond_columns,
+        class_table,
+        class_id.reshape(1, -1),
+        timestep.reshape(1, -1),
         sample_id.reshape(-1, head_width),
     )
 
@@ -425,8 +435,8 @@
     w_first_in,
     w_second_in,
     tags_in,
-    target_ref,
-    placement_ref,
+    picks_ref,
+    used_ref,
     router_ref,
     out_ref,
     stream_ref,
@@ -458,16 +468,13 @@
     back,
     router_twice,
     local_sem,
-    a_send,
-    a_recv,
-    d_send,
-    d_recv,
+    a_sem,
+    d_sem,
     z_send,
     z_recv,
     r_send,
     r_recv,
-    b_send,
-    b_recv,
+    b_sem,
 ):
     seq_index = lax.axis_index("seq")
     exp_index = lax.axis_index("exp")
@@ -500,21 +507,18 @@
             device_id_type=MESH,
         )
 
-    def attended_copy(offset):
-        peer = shifted(seq_index, offset, 1)
-        return plane_copy(
+    for offset in OFFSETS:
+        peer = seq_index ^ offset
+        plane_copy(
             attended_ref.at[rows_of(peer, tokens)],
             attended.at[seq_index],
-            a_send.at[offset],
-            a_recv.at[offset],
+            a_sem.at[0],
+            a_sem.at[1],
             peer,
-        )
-
-    for_offsets(lambda offset: attended_copy(offset).start())
-    own_attended = pltpu.make_async_copy(
-        attended_ref.at[rows_of(seq_index, tokens)], attended.at[seq_index], local_sem.at[0]
-    )
-    own_attended.start()
+        ).start()
+    pltpu.make_async_copy(
+        attended_ref.at[rows_of(seq_index, tokens)], attended.at[seq_index], a_sem.at[1]
+    ).start()
     load_mod = pltpu.make_async_copy(modulation_in, modulation_ref, local_sem.at[1])
     load_mod.start()
     load_stream = pltpu.make_async_copy(stream_in, stream_ref, local_sem.at[2])
@@ -531,12 +535,26 @@
     count = PIECES * SLOT_ROWS
     row = lax.broadcasted_iota(jnp.int32, (count, count), 0)
     column = lax.broadcasted_iota(jnp.int32, (count, count), 1)
-    by_source = ((row >> 1) & 31) * 16 + (row >> 6) * 2 + (row & 1)
+    by_source = (row & 31) * 16 + (row >> 6) * 2 + ((row >> 5) & 1)
     unmix[...] = jnp.where(by_source == column, 1.0, 0.0).astype(bf16)
-    by_piece = ((row >> 1) & 7) * SLOT_ROWS + (row >> 4) * 2 + (row & 1)
+    by_piece = ((row >> 1) & 7) * SLOT_ROWS + (row & 1) * PLANE + (row >> 4)
     mix[...] = jnp.where(by_piece == column, 1.0, 0.0).astype(bf16)
     column = lax.broadcasted_iota(jnp.int32, pick.shape, 1)
-    pick[...] = jnp.where(target_ref[...] == column, 1.0, 0.0).astype(bf16)
+    used = used_ref[...]
+    chosen = jnp.concatenate(
+        [
+            jnp.where(used > 0, picks_ref[0:1, :], -1),
+            jnp.where(used > 1, picks_ref[1:2, :], -1),
+        ],
+        axis=1,
+    ).astype(f32)
+    row = lax.broadcasted_iota(jnp.int32, (count, SLOT_ROWS), 0)
+    slot = lax.broadcasted_iota(jnp.int32, (count, SLOT_ROWS), 1)
+    mine = slot == (row & 1) * PLANE + (row >> 4)
+    token = jnp.sum(jnp.where(mine, chosen, 0.0), axis=1, keepdims=True)
+    piece = (lax.broadcasted_iota(jnp.int32, (count, 1), 0) >> 1) & 7
+    target = jnp.where(token < 0.0, -1.0, token + (piece * tokens).astype(f32))
+    pick[...] = jnp.where(column.astype(f32) == target, 1.0, 0.0).astype(bf16)
 
     load_mod.wait()
     load_stream.wait()
@@ -552,16 +570,15 @@
         )
         return carry
 
-    lax.fori_loop(0, 4 * width // 512, spread_mod, 0)
-
-    double = lax.broadcasted_iota(jnp.int32, (SLOT_ROWS, samples), 0) >> 1
+    lax.fori_loop(0, 3 * width // 512, spread_mod, 0)
+
+    double = lax.broadcasted_iota(jnp.int32, (SLOT_ROWS, samples), 0) & 31
     twice = jnp.where(
         double == lax.broadcasted_iota(jnp.int32, (SLOT_ROWS, samples), 1), 1.0, 0.0
     ).astype(bf16)
     router_twice[...] = jnp.dot(twice, router_ref[...], preferred_element_type=f32).astype(bf16)
 
-    own_attended.wait()
-    for_offsets(lambda offset: attended_copy(offset).wait_recv())
+    wait_for(attended, a_sem.at[1])
 
     def norm_rows(step, carry):
         rows = rows_of(step, 16)
@@ -578,15 +595,16 @@
 
     lax.fori_loop(0, tokens // 16, norm_rows, 0)
 
-    def dispatch_copy(half, offset):
-        peer = shifted(seq_index, offset, 1)
-        return plane_copy(
-            outgoing.at[half, rows_of(peer, 16)],
-            landed.at[half, rows_of(seq_index, 16)],
-            d_send.at[half, offset],
-            d_recv.at[half, offset],
-            peer,
-        )
+    def plane_send(source, target, sems, half):
+        place = target.at[half, rows_of(seq_index, 16)]
+        for offset in OFFSETS:
+            peer = seq_index ^ offset
+            plane_copy(
+                source.at[half, rows_of(peer, 16)], place, sems.at[half, 0], sems.at[half, 1], peer
+            ).start()
+        pltpu.make_async_copy(
+            source.at[half, rows_of(seq_index, 16)], place, sems.at[half, 1]
+        ).start()
 
     for half in range(2):
         stacked = jnp.concatenate(
@@ -597,13 +615,14 @@
             axis=0,
         )
         outgoing[half] = jnp.dot(pick[...], stacked, preferred_element_type=f32).astype(bf16)
-        for_offsets(lambda offset: dispatch_copy(half, offset).start())
-        landed[half, rows_of(seq_index, 16), :] = outgoing[half, rows_of(seq_index, 16), :]
+        plane_send(outgoing, landed, d_sem, half)
 
     logits = lax.dot_general(
         normed[...], router_twice[...], (((1,), (1,)), ((), ())), preferred_element_type=f32
     )
-    weighted = placement_ref[...] / (1.0 + jnp.exp(-logits))
+    place = lax.broadcasted_iota(jnp.int32, (tokens, SLOT_ROWS), 0).astype(f32) == chosen
+    weighted = jnp.where(place, 1.0 / (1.0 + jnp.exp(-logits)), 0.0)
+    lax.fori_loop(3 * width // 512, 4 * width // 512, spread_mod, 0)
     weight_first = weighted.astype(bf16)
     weight_rest = weighted - weight_first.astype(f32)
     weight_second = weight_rest.astype(bf16)
@@ -622,7 +641,7 @@
         )
 
     for half in range(2):
-        for_offsets(lambda offset: dispatch_copy(half, offset).wait_recv())
+        wait_for(landed.at[half], d_sem.at[half, 1])
         gathered[0, half] = jnp.dot(
             unmix[...], landed[half], preferred_element_type=f32
         ).astype(bf16)
@@ -714,16 +733,6 @@
     sum_left = ring_copy(side_sum.at[1], sum_in.at[1], r_send.at[5], r_recv.at[5], left)
     sum_left.start()
 
-    def return_copy(half, offset):
-        peer = shifted(seq_index, offset, 1)
-        return plane_copy(
-            homeward.at[half, rows_of(peer, 16)],
-            back.at[half, rows_of(seq_index, 16)],
-            b_send.at[half, offset],
-            b_recv.at[half, offset],
-            peer,
-        )
-
     for half, raw, summed in ((0, raw_left, sum_right), (1, raw_right, sum_left)):
         raw.wait_recv()
         summed.wait_recv()
@@ -734,11 +743,10 @@
             [total[:, piece * TILE : (piece + 1) * TILE] for piece in range(PIECES)], axis=0
         )
         homeward[half] = jnp.dot(mix[...], stacked, preferred_element_type=f32).astype(bf16)
-        for_offsets(lambda offset: return_copy(half, offset).start())
-        back[half, rows_of(seq_index, 16), :] = homeward[half, rows_of(seq_index, 16), :]
+        plane_send(homeward, back, b_sem, half)
 
     for half in range(2):
-        for_offsets(lambda offset: return_copy(half, offset).wait_recv())
+        wait_for(back.at[half], b_sem.at[half, 1])
         ordered = jnp.dot(unmix[...], back[half], preferred_element_type=f32).astype(bf16)
         for piece in range(PIECES):
             rows = ordered[piece * SLOT_ROWS : (piece + 1) * SLOT_ROWS, :]
@@ -750,10 +758,10 @@
             gate = token_mod[:, 3 * width + begin : 3 * width + begin + TILE]
             out_ref[:, columns] = (residual[:, columns] + gate * expert_sum).astype(bf16)
 
-    for_offsets(lambda offset: attended_copy(offset).wait_send())
+    wait_for(attended.at[pl.ds(0, PLANE - 1)], a_sem.at[0])
     for half in range(2):
-        for_offsets(lambda offset: dispatch_copy(half, offset).wait_send())
-        for_offsets(lambda offset: return_copy(half, offset).wait_send())
+        wait_for(landed.at[half, pl.ds(0, 16 * (PLANE - 1))], d_sem.at[half, 0])
+        wait_for(back.at[half, pl.ds(0, 16 * (PLANE - 1))], b_sem.at[half, 0])
     for copy in (
         own_right_0,
         own_left_1,
@@ -772,7 +780,7 @@
 
 
 def feed_forward(
-    attended_head, stream, modulation, expert_in, expert_out, query_tags, target, placement, router
+    attended_head, stream, modulation, expert_in, expert_out, query_tags, picks, used, router
 ):
     tokens, width = stream.shape
     bf16 = jnp.bfloat16
@@ -817,16 +825,13 @@
             pltpu.VMEM((2, block, TILE), bf16),
             pltpu.VMEM((SLOT_ROWS, width), bf16),
             dma((6,)),
-            dma((PLANE,)),
-            dma((PLANE,)),
-            dma((2, PLANE)),
-            dma((2, PLANE)),
+            dma((2,)),
+            dma((2, 2)),
             dma((6,)),
             dma((6,)),
             dma((6,)),
             dma((6,)),
-            dma((2, PLANE)),
-            dma((2, PLANE)),
+            dma((2, 2)),
         ],
         compiler_params=pltpu.CompilerParams(
             collective_id=1, has_side_effects=True, vmem_limit_bytes=58 * 2**20
@@ -839,8 +844,8 @@
         expert_in,
         expert_out,
         query_tags,
-        target,
-        placement,
+        picks,
+        used,
         router,
     )
 
@@ -861,31 +866,17 @@
     picked,
     counts,
 ):
-    seq_index = lax.axis_index("seq")
-    tok_local, width = stream.shape
-    column_count = class_table.shape[1]
-    half_width = width // 2
-    column = seq_index * column_count + jnp.arange(column_count, dtype=jnp.int32)
-    first_half = column < half_width
-    freq_index = jnp.where(first_half, column, column - half_width).astype(jnp.float32)
-    frequency = jnp.exp(-math.log(10000.0) * freq_index / half_width)
-    angles = timestep.astype(jnp.float32)[:, None] * frequency[None, :]
-    embedded = jnp.where(first_half[None, :], jnp.cos(angles), jnp.sin(angles))
-    table_rows = jnp.take(class_table, class_id, axis=0).astype(jnp.float32)
-    cond_columns = jax.nn.silu(embedded + table_rows).astype(jnp.bfloat16)
     head_query, keys, values, query_tags, key_tags, modulation, spans = exchange(
-        query_input, key_input, value_input, mod_weight, cond_columns, sample_id
+        query_input,
+        key_input,
+        value_input,
+        mod_weight,
+        class_table,
+        class_id,
+        timestep,
+        sample_id,
     )
     attended_head = local_attention(spans, head_query, query_tags, keys, key_tags, values)
-    slots = picked[:, 0, :]
-    expert_count, slot_total = slots.shape
-    live = jnp.arange(slot_total, dtype=jnp.int32)[None, :] < counts[:, 0][:, None]
-    chosen = jnp.where(live, slots, -1)
-    piece = jnp.arange(PIECES, dtype=jnp.int32)[None, :, None]
-    target = jnp.where(live[:, None, :], slots[:, None, :] + piece * tok_local, -1).reshape(-1, 1)
-    placement = (
-        chosen.reshape(1, -1) == jnp.arange(tok_local, dtype=jnp.int32)[:, None]
-    ).astype(jnp.float32)
     return feed_forward(
         attended_head,
         stream,
@@ -893,8 +884,8 @@
         expert_in,
         expert_out,
         query_tags,
-        target,
-        placement,
+        picked[:, 0, :].T,
+        counts.T,
         router_weight.T,
     )
 

time: 178 us -> 168 us (0.944)
  Pallas kernels: 170 us -> 165 us
  other arithmetic: 3.59 us -> 0 us
  local copies, waits for them, and re-layouts: 4.32 us -> 2.29 us
    pallas_call x1, Pallas kernels: 87.3 us -> 84.2 us  [feed_forward(): pl.pallas_call(experts_kernel, out_shape=jax.ShapeDtypeStruct((tokens, wi...]
    pallas_call x1, Pallas kernels: 62.8 us -> 60.8 us  [exchange(): pl.pallas_call(exchange_kernel, out_shape=(jax.ShapeDtypeStruct((group, h...]
    convert_element_type x3 -> x0, other arithmetic: 2.04 us -> none  [the longest x1 0.76 us: on_device(): cond_columns = jax.nn.silu(embedded + table_rows).astype(jnp.bfloat16)]
where the time goes in v4:
time: 168 us; the launch traced here: 167 us
  Pallas kernels  165 us (98%)
  local copies, waits for them, and re-layouts  2.29 us (1%)
    pallas_call x1, Pallas kernels, feed_forward(): pl.pallas_call(experts_kernel, out_shape=jax.ShapeDtypeStruct((tokens, wi...  84.2 us
    pallas_call x1, Pallas kernels, exchange(): pl.pallas_call(exchange_kernel, out_shape=(jax.ShapeDtypeStruct((group, h...  60.8 us
    pallas_call x1, Pallas kernels, local_attention(): pl.pallas_call(attention_kernel, grid_spec=pltpu.PrefetchScalarGridSpec(n...  19.8 us

profile of v4, /device:TPU:1, one launch (start us, length us, event | category | flops | bytes accessed | tf_op | source)
XLA Modules:
  0.0 167.1 jit_solution(14849823605148612011)
XLA Ops:
  0.0 60.8 %exchange.1 = (bf16[4096,128]{1,0:T(8,128)(2,1)}, bf16[6144,128]{1,0:T(8,128)(2,1)}, bf16[6144,128]{1,0:T(8,128)(2,1)}, bf16[4096,128]{1,0:T(8,128)(2,1)}, bf16[...) custom-call(bf16[128,4096]{1,0:T(8,128)(2,1)} %query_in.1, bf16[128,4096]{1,0:T(8,128)(2,1)} %key_in.1, ...), custom_call_target="tpu_custom_call" | custom-call | tf_op jit(solution)/shard_map/exchange/pallas_call | solution.py:386
  60.8 19.8 %attention.1.attended_ref = bf16[4096,128]{1,0:T(8,128)(2,1)} custom-call(s32[8,128]{1,0:T(8,128)} %get-tuple-element.12.spans, bf16[4096,128]{1,0:T(8,128)(2,1)} %get-tuple-element.13.q_ref, bf16[4096,128]{1,0:T(8,128)(2,1)} %get-tuple-element.14.fq_ref.tags_in, bf16[6144,128]{1,0:T(8,128)(2,1)} %get-tuple-element.15.k_ref, ...), custom_call_target="tpu_custom_call" | custom-call | tf_op jit(solution)/shard_map/attention/pallas_call | solution.py:58
  80.6 84.2 %experts.1 = bf16[128,4096]{1,0:T(8,128)(2,1)} custom-call(bf16[4096,128]{1,0:T(8,128)(2,1)} %attention.1.attended_ref, bf16[128,4096]{1,0:T(8,128)(2,1)} %stream_in.1, bf16[128,32,128]{2,1,0:T(8,128)(2,1)} %get-tuple-element.18.modulation_in, bf16[1,4096,1024]{2,1,0:T(8,128)(2,1)} %w_first_in.1, bf16[1,1024,4096]{2,1,0:T(8,128)(2,1)} %w_second_in.1, ...), custom_call_target="tpu_custom_call" | custom-call | tf_op jit(solution)/shard_map/experts/pallas_call | solution.py:793
  164.8 2.3 %copy.16 = bf16[128,4096]{1,0:T(8,128)(2,1)} copy(bf16[128,4096]{1,0:T(8,128)(2,1)} %experts.1) | data formatting | bytes 2097152

commit v5 on v4

--- a/solution.py
+++ b/solution.py
@@ -13,7 +13,8 @@
 EPS = 1e-06
 
 
-Q_ROWS = 256
+Q_ROWS = 512
+KEY_STEP = 256
 FAR = 32768.0
 
 
@@ -23,29 +24,34 @@
     parts = spans[1, step]
     head_width = q_ref.shape[1]
     factor = math.log2(math.e) / math.sqrt(head_width)
-    most_parts = (2 * MOST + Q_ROWS) // Q_ROWS + 1
+    least_parts = Q_ROWS // KEY_STEP
+    most_parts = (2 * MOST + Q_ROWS) // KEY_STEP + 1
 
     def with_parts(number):
-        span = number * Q_ROWS
+        span = number * KEY_STEP
 
         @pl.when(parts == number)
         def _():
             first = pl.multiple_of(jnp.minimum(start, k_ref.shape[0] - span), 128)
             rows = pl.ds(first, span)
-            query = jnp.concatenate([q_ref[...], fq_ref[...]], axis=1)
             keys = jnp.concatenate([k_ref[rows, :], fk_ref[rows, :]], axis=1)
-            scores = lax.dot_general(
-                query, keys, (((1,), (1,)), ((), ())), preferred_element_type=jnp.float32
-            )
-            highest = jnp.max(scores, axis=1, keepdims=True)
-            numer = jnp.exp2((scores - highest) * factor).astype(jnp.bfloat16)
             values = jnp.concatenate(
                 [v_ref[rows, :], jnp.ones((span, head_width), jnp.bfloat16)], axis=1
             )
-            total = jnp.dot(numer, values, preferred_element_type=jnp.float32)
-            out_ref[...] = (total[:, :head_width] / total[:, head_width:]).astype(jnp.bfloat16)
-
-    for number in range(2, most_parts + 1):
+            for line in range(0, Q_ROWS, KEY_STEP):
+                lines = slice(line, line + KEY_STEP)
+                query = jnp.concatenate([q_ref[lines, :], fq_ref[lines, :]], axis=1)
+                scores = lax.dot_general(
+                    query, keys, (((1,), (1,)), ((), ())), preferred_element_type=jnp.float32
+                )
+                highest = jnp.max(scores, axis=1, keepdims=True)
+                numer = jnp.exp2((scores - highest) * factor).astype(jnp.bfloat16)
+                total = jnp.dot(numer, values, preferred_element_type=jnp.float32)
+                out_ref[lines, :] = (total[:, :head_width] / total[:, head_width:]).astype(
+                    jnp.bfloat16
+                )
+
+    for number in range(least_parts, most_parts + 1):
         with_parts(number)
 
 
@@ -163,10 +169,10 @@
 
     arrays = ((key_in, key_out, MOST), (value_in, value_out, MOST), (query_in, query_out, 0))
 
-    def send_heads(which):
+    def send_heads(which, part):
         source, target, before = arrays[which]
         place = target.at[pl.ds(pl.multiple_of(before + seq_index * tokens, tokens), tokens)]
-        for offset in OFFSETS:
+        for offset in OFFSETS[part::2]:
             peer = seq_index ^ offset
             copy_to(
                 source.at[:, rows_of(peer, head_width)],
@@ -176,9 +182,10 @@
                 peer,
                 exp_index,
             ).start()
-        pltpu.make_async_copy(
-            source.at[:, rows_of(seq_index, head_width)], place, p_recv.at[which]
-        ).start()
+        if part == 0:
+            pltpu.make_async_copy(
+                source.at[:, rows_of(seq_index, head_width)], place, p_recv.at[which]
+            ).start()
 
     def wait_heads(which):
         _, target, before = arrays[which]
@@ -236,7 +243,7 @@
         for copy in modulation_copies(phase):
             copy.wait_recv()
 
-    send_heads(0)
+    send_heads(0, 0)
     load_weight = pltpu.make_async_copy(weight_in, weight, local_sem.at[0])
     load_weight.start()
 
@@ -275,6 +282,7 @@
             exp_index,
         ).start()
     pltpu.make_async_copy(own_condition, conditions.at[seq_index], c_sem.at[1]).start()
+    send_heads(0, 1)
     wait_for(conditions, c_sem.at[1])
     load_weight.wait()
     condition = jnp.concatenate([conditions[place] for place in range(PLANE)], axis=1)
@@ -282,7 +290,7 @@
     keep = pltpu.make_async_copy(own_modulation, modulation_out.at[slot], local_sem.at[4])
     keep.start()
     send_modulation(0)
-    send_heads(1)
+    send_heads(1, 0)
 
     ids = ids_ref[...]
     lane = lax.broadcasted_iota(jnp.int32, (1, head_width), 1)
@@ -323,6 +331,19 @@
     keep_key_tags.start()
     keep_query_tags = pltpu.make_async_copy(query_tags, query_tags_out, local_sem.at[6])
     keep_query_tags.start()
+
+    keep.wait()
+    wait_modulation(0)
+    send_modulation(1)
+    send_heads(1, 1)
+    wait_modulation(1)
+    send_modulation(2)
+    wait_heads(0)
+    for copy in halo_copies(0):
+        copy.start()
+    send_heads(2, 0)
+    wait_modulation(2)
+    send_modulation(3)
 
     low = jnp.zeros((1, head_width), f32)
     high = jnp.zeros((1, head_width), f32)
@@ -334,25 +355,15 @@
         high = high + jnp.where(lane == block, total(ids <= last), 0.0)
     low = (low.astype(jnp.int32) - first_token + MOST) & ~127
     high = high.astype(jnp.int32) - first_token + MOST
-    parts = jnp.maximum((high - low + Q_ROWS - 1) >> 8, 2)
+    parts = jnp.maximum((high - low + KEY_STEP - 1) // KEY_STEP, Q_ROWS // KEY_STEP)
     spans_out[...] = jnp.where(
         lax.broadcasted_iota(jnp.int32, spans_out.shape, 0) == 0, low, parts
     )
 
-    keep.wait()
-    wait_modulation(0)
-    send_modulation(1)
-    wait_modulation(1)
-    send_modulation(2)
-    wait_heads(0)
-    for copy in halo_copies(0):
-        copy.start()
-    send_heads(2)
-    wait_modulation(2)
-    send_modulation(3)
     wait_heads(1)
     for copy in halo_copies(1):
         copy.start()
+    send_heads(2, 1)
     wait_heads(2)
     wait_modulation(3)
     keep_key_tags.wait()

time: 168 us -> 161 us (0.958)
  Pallas kernels: 165 us -> 159 us
    pallas_call x1, Pallas kernels: 19.8 us -> 16.5 us  [local_attention(): pl.pallas_call(attention_kernel, grid_spec=pltpu.PrefetchScalarGridSpec(n...]
    pallas_call x1, Pallas kernels: 84.2 us -> 81.2 us  [feed_forward(): pl.pallas_call(experts_kernel, out_shape=jax.ShapeDtypeStruct((tokens, wi...]
where the time goes in v5:
time: 161 us
  Pallas kernels  159 us (99%)
  local copies, waits for them, and re-layouts  2.29 us (1%)
    pallas_call x1, Pallas kernels, feed_forward(): pl.pallas_call(experts_kernel, out_shape=jax.ShapeDtypeStruct((tokens, wi...  81.2 us
    pallas_call x1, Pallas kernels, exchange(): pl.pallas_call(exchange_kernel, out_shape=(jax.ShapeDtypeStruct((group, h...  60.9 us
    pallas_call x1, Pallas kernels, local_attention(): pl.pallas_call(attention_kernel, grid_spec=pltpu.PrefetchScalarGridSpec(n...  16.5 us

profile of v5, /device:TPU:1, one launch (start us, length us, event | category | flops | bytes accessed | tf_op | source)
XLA Modules:
  0.0 160.9 jit_solution(3217661360722440802)
XLA Ops:
  0.0 60.9 %exchange.1 = (bf16[4096,128]{1,0:T(8,128)(2,1)}, bf16[6144,128]{1,0:T(8,128)(2,1)}, bf16[6144,128]{1,0:T(8,128)(2,1)}, bf16[4096,128]{1,0:T(8,128)(2,1)}, bf16[...) custom-call(bf16[128,4096]{1,0:T(8,128)(2,1)} %query_in.1, bf16[128,4096]{1,0:T(8,128)(2,1)} %key_in.1, ...), custom_call_target="tpu_custom_call" | custom-call | tf_op jit(solution)/shard_map/exchange/pallas_call | solution.py:397
  60.9 16.5 %attention.1.attended_ref = bf16[4096,128]{1,0:T(8,128)(2,1)} custom-call(s32[8,128]{1,0:T(8,128)} %get-tuple-element.12.spans, bf16[4096,128]{1,0:T(8,128)(2,1)} %get-tuple-element.13.q_ref, bf16[4096,128]{1,0:T(8,128)(2,1)} %get-tuple-element.14.fq_ref.tags_in, bf16[6144,128]{1,0:T(8,128)(2,1)} %get-tuple-element.15.k_ref, ...), custom_call_target="tpu_custom_call" | custom-call | tf_op jit(solution)/shard_map/attention/pallas_call | solution.py:64
  77.4 81.2 %experts.1 = bf16[128,4096]{1,0:T(8,128)(2,1)} custom-call(bf16[4096,128]{1,0:T(8,128)(2,1)} %attention.1.attended_ref, bf16[128,4096]{1,0:T(8,128)(2,1)} %stream_in.1, bf16[128,32,128]{2,1,0:T(8,128)(2,1)} %get-tuple-element.18.modulation_in, bf16[1,4096,1024]{2,1,0:T(8,128)(2,1)} %w_first_in.1, bf16[1,1024,4096]{2,1,0:T(8,128)(2,1)} %w_second_in.1, ...), custom_call_target="tpu_custom_call" | custom-call | tf_op jit(solution)/shard_map/experts/pallas_call | solution.py:804
  158.6 2.3 %copy.16 = bf16[128,4096]{1,0:T(8,128)(2,1)} copy(bf16[128,4096]{1,0:T(8,128)(2,1)} %experts.1) | data formatting | bytes 2097152

commit v6 on v5

--- a/solution.py
+++ b/solution.py
@@ -89,7 +89,19 @@
 SLOT_ROWS = 64
 
 
-OFFSETS = sorted(range(1, PLANE), key=lambda offset: (offset * 13) % PLANE)
+OFFSETS = [(number * 13) % PLANE for number in range(1, PLANE)]
+
+
+def mirrored(offset):
+    other = (0, 3, 2, 1)
+    return other[offset // 8] * 8 + other[offset // 2 % 4] * 2 + offset % 2
+
+
+def partners(seq_index, offsets):
+    core = seq_index % 2
+    return [
+        seq_index ^ (offset + core * (mirrored(offset) - offset)) for offset in offsets
+    ]
 
 
 def greet(seq_index, exp_index, ring):
@@ -172,8 +184,7 @@
     def send_heads(which, part):
         source, target, before = arrays[which]
         place = target.at[pl.ds(pl.multiple_of(before + seq_index * tokens, tokens), tokens)]
-        for offset in OFFSETS[part::2]:
-            peer = seq_index ^ offset
+        for peer in partners(seq_index, OFFSETS[15:] if part else OFFSETS[:15]):
             copy_to(
                 source.at[:, rows_of(peer, head_width)],
                 place,
@@ -272,13 +283,13 @@
     value = embedded + table_rows
     own_condition[...] = (value / (1.0 + jnp.exp(-value))).astype(bf16)
 
-    for offset in OFFSETS:
+    for peer in partners(seq_index, OFFSETS):
         copy_to(
             own_condition,
             conditions.at[seq_index],
             c_sem.at[0],
             c_sem.at[1],
-            seq_index ^ offset,
+            peer,
             exp_index,
         ).start()
     pltpu.make_async_copy(own_condition, conditions.at[seq_index], c_sem.at[1]).start()
@@ -336,14 +347,12 @@
     wait_modulation(0)
     send_modulation(1)
     send_heads(1, 1)
-    wait_modulation(1)
-    send_modulation(2)
     wait_heads(0)
     for copy in halo_copies(0):
         copy.start()
     send_heads(2, 0)
-    wait_modulation(2)
-    send_modulation(3)
+    wait_modulation(1)
+    send_modulation(2)
 
     low = jnp.zeros((1, head_width), f32)
     high = jnp.zeros((1, head_width), f32)
@@ -364,6 +373,8 @@
     for copy in halo_copies(1):
         copy.start()
     send_heads(2, 1)
+    wait_modulation(2)
+    send_modulation(3)
     wait_heads(2)
     wait_modulation(3)
     keep_key_tags.wait()
@@ -518,8 +529,7 @@
             device_id_type=MESH,
         )
 
-    for offset in OFFSETS:
-        peer = seq_index ^ offset
+    for peer in partners(seq_index, OFFSETS):
         plane_copy(
             attended_ref.at[rows_of(peer, tokens)],
             attended.at[seq_index],
@@ -608,8 +618,7 @@
 
     def plane_send(source, target, sems, half):
         place = target.at[half, rows_of(seq_index, 16)]
-        for offset in OFFSETS:
-            peer = seq_index ^ offset
+        for peer in partners(seq_index, OFFSETS):
             plane_copy(
                 source.at[half, rows_of(peer, 16)], place, sems.at[half, 0], sems.at[half, 1], peer
             ).start()
@@ -651,36 +660,35 @@
             )
         )
 
+    ring_copies = []
     for half in range(2):
         wait_for(landed.at[half], d_sem.at[half, 1])
         gathered[0, half] = jnp.dot(
             unmix[...], landed[half], preferred_element_type=f32
         ).astype(bf16)
-        if half == 0:
-            own_right_0 = ring_copy(
-                gathered.at[0, 0], gathered.at[2, 0], z_send.at[0], z_recv.at[0], right
-            )
-            own_right_0.start()
-        else:
-            own_left_1 = ring_copy(
-                gathered.at[0, 1], gathered.at[3, 1], z_send.at[1], z_recv.at[1], left
-            )
-            own_left_1.start()
+        to_right = ring_copy(
+            gathered.at[0, half], gathered.at[2, half], z_send.at[half], z_recv.at[half], right
+        )
+        to_right.start()
+        to_left = ring_copy(
+            gathered.at[0, half],
+            gathered.at[3, half],
+            z_send.at[2 + half],
+            z_recv.at[2 + half],
+            left,
+        )
+        to_left.start()
+        ring_copies += [to_right, to_left]
         line_up(0, half)
+    own_right_0, own_left_0, own_right_1, own_left_1 = ring_copies
     own_right_0.wait_recv()
     on_right_0 = ring_copy(
-        gathered.at[2, 0], gathered.at[1, 0], z_send.at[2], z_recv.at[2], right
+        gathered.at[2, 0], gathered.at[1, 0], z_send.at[4], z_recv.at[4], right
     )
     on_right_0.start()
     own_left_1.wait_recv()
-    on_left_1 = ring_copy(gathered.at[3, 1], gathered.at[1, 1], z_send.at[3], z_recv.at[3], left)
+    on_left_1 = ring_copy(gathered.at[3, 1], gathered.at[1, 1], z_send.at[5], z_recv.at[5], left)
     on_left_1.start()
-    own_right_1 = ring_copy(
-        gathered.at[0, 1], gathered.at[2, 1], z_send.at[4], z_recv.at[4], right
-    )
-    own_right_1.start()
-    own_left_0 = ring_copy(gathered.at[0, 0], gathered.at[3, 0], z_send.at[5], z_recv.at[5], left)
-    own_left_0.start()
     line_up(2, 0)
     line_up(3, 1)
     load_first.wait()
@@ -713,6 +721,17 @@
 
         lax.fori_loop(0, HALF // 256, columns_of, 0)
 
+    own_left_0.wait_recv()
+    line_up(3, 0)
+    own_right_1.wait_recv()
+    line_up(2, 1)
+    first_product(2 * SLOT_ROWS)
+    second_product(2 * SLOT_ROWS, 0, side_raw.at[0], held.at[0])
+    raw_left = ring_copy(side_raw.at[0], raw_in.at[0], r_send.at[2], r_recv.at[2], left)
+    raw_left.start()
+    second_product(2 * SLOT_ROWS, 1, held.at[1], side_raw.at[1])
+    raw_right = ring_copy(side_raw.at[1], raw_in.at[1], r_send.at[3], r_recv.at[3], right)
+    raw_right.start()
     on_right_0.wait_recv()
     line_up(1, 0)
     on_left_1.wait_recv()
@@ -724,17 +743,6 @@
     second_product(0, 1, own_total.at[1], far_out.at[1])
     far_left = ring_copy(far_out.at[1], far_in.at[1], r_send.at[1], r_recv.at[1], left)
     far_left.start()
-    own_right_1.wait_recv()
-    line_up(2, 1)
-    own_left_0.wait_recv()
-    line_up(3, 0)
-    first_product(2 * SLOT_ROWS)
-    second_product(2 * SLOT_ROWS, 0, side_raw.at[0], held.at[0])
-    raw_left = ring_copy(side_raw.at[0], raw_in.at[0], r_send.at[2], r_recv.at[2], left)
-    raw_left.start()
-    second_product(2 * SLOT_ROWS, 1, held.at[1], side_raw.at[1])
-    raw_right = ring_copy(side_raw.at[1], raw_in.at[1], r_send.at[3], r_recv.at[3], right)
-    raw_right.start()
     far_right.wait_recv()
     side_sum[0] = (held[0] + far_in[0].astype(f32)).astype(bf16)
     sum_right = ring_copy(side_sum.at[0], sum_in.at[0], r_send.at[4], r_recv.at[4], right)

time: 161 us -> 151 us (0.938)
  Pallas kernels: 159 us -> 150 us
    pallas_call x1, Pallas kernels: 60.9 us -> 54.1 us  [exchange(): pl.pallas_call(exchange_kernel, out_shape=(jax.ShapeDtypeStruct((group, h...]
    pallas_call x1, Pallas kernels: 81.2 us -> 78.3 us  [feed_forward(): pl.pallas_call(experts_kernel, out_shape=jax.ShapeDtypeStruct((tokens, wi...]
where the time goes in v6:
time: 151 us; the launch traced here: 152 us
  Pallas kernels  150 us (99%)
  local copies, waits for them, and re-layouts  2.29 us (2%)
    pallas_call x1, Pallas kernels, feed_forward(): pl.pallas_call(experts_kernel, out_shape=jax.ShapeDtypeStruct((tokens, wi...  78.3 us
    pallas_call x1, Pallas kernels, exchange(): pl.pallas_call(exchange_kernel, out_shape=(jax.ShapeDtypeStruct((group, h...  54.1 us
    pallas_call x1, Pallas kernels, local_attention(): pl.pallas_call(attention_kernel, grid_spec=pltpu.PrefetchScalarGridSpec(n...  17.1 us

profile of v6, /device:TPU:1, one launch (start us, length us, event | category | flops | bytes accessed | tf_op | source)
XLA Modules:
  0.0 151.8 jit_solution(15034762436696590555)
XLA Ops:
  0.0 54.1 %exchange.1 = (bf16[4096,128]{1,0:T(8,128)(2,1)}, bf16[6144,128]{1,0:T(8,128)(2,1)}, bf16[6144,128]{1,0:T(8,128)(2,1)}, bf16[4096,128]{1,0:T(8,128)(2,1)}, bf16[...) custom-call(bf16[128,4096]{1,0:T(8,128)(2,1)} %query_in.1, bf16[128,4096]{1,0:T(8,128)(2,1)} %key_in.1, ...), custom_call_target="tpu_custom_call" | custom-call | tf_op jit(solution)/shard_map/exchange/pallas_call | solution.py:408
  54.2 17.1 %attention.1.attended_ref = bf16[4096,128]{1,0:T(8,128)(2,1)} custom-call(s32[8,128]{1,0:T(8,128)} %get-tuple-element.12.spans, bf16[4096,128]{1,0:T(8,128)(2,1)} %get-tuple-element.13.q_ref, bf16[4096,128]{1,0:T(8,128)(2,1)} %get-tuple-element.14.fq_ref.tags_in, bf16[6144,128]{1,0:T(8,128)(2,1)} %get-tuple-element.15.k_ref, ...), custom_call_target="tpu_custom_call" | custom-call | tf_op jit(solution)/shard_map/attention/pallas_call | solution.py:64
  71.3 78.3 %experts.1 = bf16[128,4096]{1,0:T(8,128)(2,1)} custom-call(bf16[4096,128]{1,0:T(8,128)(2,1)} %attention.1.attended_ref, bf16[128,4096]{1,0:T(8,128)(2,1)} %stream_in.1, bf16[128,32,128]{2,1,0:T(8,128)(2,1)} %get-tuple-element.18.modulation_in, bf16[1,4096,1024]{2,1,0:T(8,128)(2,1)} %w_first_in.1, bf16[1,1024,4096]{2,1,0:T(8,128)(2,1)} %w_second_in.1, ...), custom_call_target="tpu_custom_call" | custom-call | tf_op jit(solution)/shard_map/experts/pallas_call | solution.py:812
  149.6 2.3 %copy.16 = bf16[128,4096]{1,0:T(8,128)(2,1)} copy(bf16[128,4096]{1,0:T(8,128)(2,1)} %experts.1) | data formatting | bytes 2097152

commit v7 on v6

--- a/solution.py
+++ b/solution.py
@@ -89,7 +89,7 @@
 SLOT_ROWS = 64
 
 
-OFFSETS = [(number * 13) % PLANE for number in range(1, PLANE)]
+OFFSETS = [(number * 5) % PLANE for number in range(1, PLANE)]
 
 
 def mirrored(offset):
@@ -233,14 +233,10 @@
             source = modulation_out.at[rows_of(slot // 4, 4)]
             target = source
             places = [((((at_y + d) % 4) * 4 + at_x) * 2 + core, exp_index) for d in (1, 2, 3)]
-        elif phase == 2:
+        else:
             source = modulation_out.at[rows_of(slot // 16, 16)]
             target = source
             places = [(seq_index, (exp_index + d) % 4) for d in (1, 2, 3)]
-        else:
-            source = modulation_out.at[rows_of(core, 64)]
-            target = source
-            places = [(at_y * 8 + at_x * 2 + 1 - core, exp_index)]
         return [
             copy_to(source, target, m_send.at[phase, i], m_recv.at[phase, i], peer, other)
             for i, (peer, other) in enumerate(places)
@@ -373,10 +369,8 @@
     for copy in halo_copies(1):
         copy.start()
     send_heads(2, 1)
+    wait_heads(2)
     wait_modulation(2)
-    send_modulation(3)
-    wait_heads(2)
-    wait_modulation(3)
     keep_key_tags.wait()
     keep_query_tags.wait()
     for which in range(2):
@@ -388,7 +382,7 @@
     for which in range(2):
         for copy in halo_copies(which):
             copy.wait_send()
-    for phase in range(4):
+    for phase in range(3):
         for copy in modulation_copies(phase):
             copy.wait_send()
 
@@ -431,8 +425,8 @@
             dma((3,)),
             dma((2, 2)),
             dma((2, 2)),
-            dma((4, 3)),
-            dma((4, 3)),
+            dma((3, 3)),
+            dma((3, 3)),
         ],
         compiler_params=pltpu.CompilerParams(
             collective_id=0, has_side_effects=True, vmem_limit_bytes=60 * 2**20
@@ -490,6 +484,7 @@
     back,
     router_twice,
     local_sem,
+    s_sem,
     a_sem,
     d_sem,
     z_send,
@@ -529,6 +524,19 @@
             device_id_type=MESH,
         )
 
+    own_half = rows_of(seq_index % 2, modulation_ref.shape[0] // 2)
+    load_mod = pltpu.make_async_copy(
+        modulation_in.at[own_half], modulation_ref.at[own_half], local_sem.at[1]
+    )
+    load_mod.start()
+    share_mod = plane_copy(
+        modulation_in.at[own_half],
+        modulation_ref.at[own_half],
+        s_sem.at[0],
+        s_sem.at[1],
+        seq_index ^ 1,
+    )
+    share_mod.start()
     for peer in partners(seq_index, OFFSETS):
         plane_copy(
             attended_ref.at[rows_of(peer, tokens)],
@@ -540,8 +548,6 @@
     pltpu.make_async_copy(
         attended_ref.at[rows_of(seq_index, tokens)], attended.at[seq_index], a_sem.at[1]
     ).start()
-    load_mod = pltpu.make_async_copy(modulation_in, modulation_ref, local_sem.at[1])
-    load_mod.start()
     load_stream = pltpu.make_async_copy(stream_in, stream_ref, local_sem.at[2])
     load_stream.start()
     load_tags = pltpu.make_async_copy(
@@ -578,6 +584,7 @@
     pick[...] = jnp.where(column.astype(f32) == target, 1.0, 0.0).astype(bf16)
 
     load_mod.wait()
+    share_mod.wait_recv()
     load_stream.wait()
 
     load_tags.wait()
@@ -777,6 +784,7 @@
             gate = token_mod[:, 3 * width + begin : 3 * width + begin + TILE]
             out_ref[:, columns] = (residual[:, columns] + gate * expert_sum).astype(bf16)
 
+    share_mod.wait_send()
     wait_for(attended.at[pl.ds(0, PLANE - 1)], a_sem.at[0])
     for half in range(2):
         wait_for(landed.at[half, pl.ds(0, 16 * (PLANE - 1))], d_sem.at[half, 0])
@@ -845,6 +853,7 @@
             pltpu.VMEM((SLOT_ROWS, width), bf16),
             dma((6,)),
             dma((2,)),
+            dma((2,)),
             dma((2, 2)),
             dma((6,)),
             dma((6,)),

time: 151 us -> 153 us (1.013)
    pallas_call x1, Pallas kernels: 78.3 us -> 80.3 us  [feed_forward(): pl.pallas_call(experts_kernel, out_shape=jax.ShapeDtypeStruct((tokens, wi...]
where the time goes in v7:
time: 153 us; the launch traced here: 152 us
  Pallas kernels  150 us (98%)
  local copies, waits for them, and re-layouts  2.29 us (1%)
    pallas_call x1, Pallas kernels, feed_forward(): pl.pallas_call(experts_kernel, out_shape=jax.ShapeDtypeStruct((tokens, wi...  80.3 us
    pallas_call x1, Pallas kernels, exchange(): pl.pallas_call(exchange_kernel, out_shape=(jax.ShapeDtypeStruct((group, h...  53.4 us
    pallas_call x1, Pallas kernels, local_attention(): pl.pallas_call(attention_kernel, grid_spec=pltpu.PrefetchScalarGridSpec(n...  16.3 us

profile of v7, /device:TPU:1, one launch (start us, length us, event | category | flops | bytes accessed | tf_op | source)
XLA Modules:
  0.0 152.4 jit_solution(13819724018751617493)
XLA Ops:
  0.0 53.4 %exchange.1 = (bf16[4096,128]{1,0:T(8,128)(2,1)}, bf16[6144,128]{1,0:T(8,128)(2,1)}, bf16[6144,128]{1,0:T(8,128)(2,1)}, bf16[4096,128]{1,0:T(8,128)(2,1)}, bf16[...) custom-call(bf16[128,4096]{1,0:T(8,128)(2,1)} %query_in.1, bf16[128,4096]{1,0:T(8,128)(2,1)} %key_in.1, ...), custom_call_target="tpu_custom_call" | custom-call | tf_op jit(solution)/shard_map/exchange/pallas_call | solution.py:402
  53.4 16.3 %attention.1.attended_ref = bf16[4096,128]{1,0:T(8,128)(2,1)} custom-call(s32[8,128]{1,0:T(8,128)} %get-tuple-element.12.spans, bf16[4096,128]{1,0:T(8,128)(2,1)} %get-tuple-element.13.q_ref, bf16[4096,128]{1,0:T(8,128)(2,1)} %get-tuple-element.14.fq_ref.tags_in, bf16[6144,128]{1,0:T(8,128)(2,1)} %get-tuple-element.15.k_ref, ...), custom_call_target="tpu_custom_call" | custom-call | tf_op jit(solution)/shard_map/attention/pallas_call | solution.py:64
  69.8 80.3 %experts.1 = bf16[128,4096]{1,0:T(8,128)(2,1)} custom-call(bf16[4096,128]{1,0:T(8,128)(2,1)} %attention.1.attended_ref, bf16[128,4096]{1,0:T(8,128)(2,1)} %stream_in.1, bf16[128,32,128]{2,1,0:T(8,128)(2,1)} %get-tuple-element.18.modulation_in, bf16[1,4096,1024]{2,1,0:T(8,128)(2,1)} %w_first_in.1, bf16[1,1024,4096]{2,1,0:T(8,128)(2,1)} %w_second_in.1, ...), custom_call_target="tpu_custom_call" | custom-call | tf_op jit(solution)/shard_map/experts/pallas_call | solution.py:820
  150.1 2.3 %copy.16 = bf16[128,4096]{1,0:T(8,128)(2,1)} copy(bf16[128,4096]{1,0:T(8,128)(2,1)} %experts.1) | data formatting | bytes 2097152
